TPU v7x, 32 devices: a whole 2x2x4 slice. The times are simulated.
32 devices in a mesh: db: 16 (over z, y, x), head: 2 (over core).
Axes of the slice: x: 2, y: 2, z: 4, core: 2. Of those that a mesh axis runs over, the one named last changes fastest.
Arguments:
- queries: bfloat16 [2048, 4096], P('db', 'head'), may hold values from -6 to 6
- w_key: bfloat16 [896, 4096], P(None, 'head'), may hold values from -0.1875 to 0.1875
- w_value: bfloat16 [896, 4096], P(None, 'head'), may hold values from -0.1875 to 0.1875
- w_out: bfloat16 [4096, 4096], P('head'), may hold values from -0.375 to 0.375
- encodings: bfloat16 [1024, 128, 896], P('db', 'head'), may hold values from -6 to 6
- nbr_row: int32 [32, 8], P('db'), may hold values from 0 to 63
- nbr_owner: int32 [32, 8], P('db'), may hold values from 0 to 15, all different within a row; in each aligned block of 2 rows (0 to 1, 2 to 3, ...) at most 2 rows name the same one
- nbr_count: int32 [32], P('db'), may hold values from 2 to 8
- grad_out: bfloat16 [2048, 4096], P('db', 'head'), may hold values from -6 to 6
Outputs:
- attended: bfloat16 [2048, 4096], P('db', 'head')
- grad_queries: bfloat16 [2048, 4096], P('db', 'head')
- grad_wk: float32 [896, 4096], P('db', 'head')
- grad_wv: float32 [896, 4096], P('db', 'head')
- grad_wo: float32 [4096, 4096], P('head', 'db')
Inputs may be any that keep to these rules, and one draw needn't show every extreme that they name: `nbr_owner`: the 8 owners named by one group are all different.
All inputs are finite; a program needn't handle non-finite values.
Results may differ from a plain program's by a relative error of at most 0.023.
Values may be sent and summed in bfloat16 or wider, within the bound.
A program may use at most 192 MiB of HBM per device.

v0:
```python
import math

import jax
import jax.numpy as jnp
from jax import lax
from jax.sharding import PartitionSpec as P

HD = 128


def shards(queries, w_key, w_value, w_out, encodings, nbr_row, nbr_owner, nbr_count, grad_out):
    db_count = lax.axis_size("db")
    head_count = lax.axis_size("head")
    groups, slot_count = nbr_row.shape
    tok_rows, local_width = queries.shape
    group_len = tok_rows // groups
    enc_width = encodings.shape[2]
    slice_len = encodings.shape[1]
    local_heads = local_width // HD
    factor = 1.0 / math.sqrt(HD)
    owner_ids = lax.broadcasted_iota(jnp.int32, (1, 1, db_count), 2)
    chosen = nbr_owner[:, :, None] == owner_ids
    wanted = jnp.sum(jnp.where(chosen, nbr_row[:, :, None], 0), axis=1)
    incoming = lax.all_to_all(wanted, "db", split_axis=1, concat_axis=1, tiled=True)
    table = jnp.take(encodings, incoming, axis=0)
    selector = chosen.astype(jnp.bfloat16)
    spread = jnp.broadcast_to(
        table[:, :, None], (groups, db_count, head_count, slice_len, enc_width)
    )
    spread = spread.reshape(groups, db_count * head_count * slice_len, enc_width)
    received = lax.all_to_all(spread, ("db", "head"), split_axis=1, concat_axis=1, tiled=True)
    received = received.reshape(groups, db_count, head_count * slice_len, enc_width)
    slots = jnp.einsum(
        "ckn,cnte->ckte", selector, received, preferred_element_type=jnp.float32
    ).astype(jnp.bfloat16)
    keys = jnp.einsum("cste,ef->cstf", slots, w_key, preferred_element_type=jnp.float32).astype(
        jnp.bfloat16
    )
    values = jnp.einsum("cste,ef->cstf", slots, w_value, preferred_element_type=jnp.float32).astype(
        jnp.bfloat16
    )
    keys, values = (keys, values)
    key_len = slot_count * keys.shape[2]
    query_heads = queries.reshape(groups, group_len, local_heads, HD)
    key_heads = keys.reshape(groups, key_len, local_heads, HD)
    value_heads = values.reshape(groups, key_len, local_heads, HD)
    scores = (
        jnp.einsum("cqhd,ckhd->chqk", query_heads, key_heads, preferred_element_type=jnp.float32)
        * factor
    )
    key_slot = lax.broadcasted_iota(jnp.int32, (1, key_len), 1) // keys.shape[2]
    live = key_slot < nbr_count[:, None]
    expo = jnp.where(live[:, None, None, :], jnp.exp(scores), jnp.float32(0.0))
    probs = expo / jnp.sum(expo, axis=-1, keepdims=True)
    probs_b = probs.astype(jnp.bfloat16)
    mixed = jnp.einsum("chqk,ckhd->cqhd", probs_b, value_heads, preferred_element_type=jnp.float32)
    mixed = mixed.astype(jnp.bfloat16).reshape(tok_rows, local_width)
    out_term = jnp.dot(mixed, w_out, preferred_element_type=jnp.float32)
    attended = lax.psum_scatter(
        out_term.astype(jnp.bfloat16), "head", scatter_dimension=1, tiled=True
    )
    piece = lax.all_gather(grad_out, "head", axis=1, tiled=True)
    acc_mixed = lax.dot_general(
        piece, w_out, (((1,), (1,)), ((), ())), preferred_element_type=jnp.float32
    )
    block = lax.dot_general(
        mixed, piece, (((0,), (0,)), ((), ())), preferred_element_type=jnp.float32
    )
    out_grad = block
    acc_mixed, out_grad = (acc_mixed, out_grad)
    grad_wo = lax.psum_scatter(
        out_grad.astype(jnp.bfloat16), "db", scatter_dimension=1, tiled=True
    ).astype(jnp.float32)
    d_mixed = acc_mixed.astype(jnp.bfloat16).reshape(groups, group_len, local_heads, HD)
    d_probs = jnp.einsum(
        "cqhd,ckhd->chqk", d_mixed, value_heads, preferred_element_type=jnp.float32
    )
    inner = jnp.sum(probs * d_probs, axis=-1, keepdims=True)
    d_scores = (probs * (d_probs - inner) * factor).astype(jnp.bfloat16)
    grad_queries = jnp.einsum(
        "chqk,ckhd->cqhd", d_scores, key_heads, preferred_element_type=jnp.float32
    )
    grad_queries = grad_queries.astype(jnp.bfloat16).reshape(tok_rows, local_width)
    d_keys = jnp.einsum(
        "chqk,cqhd->ckhd", d_scores, query_heads, preferred_element_type=jnp.float32
    ).astype(jnp.bfloat16)
    d_values = jnp.einsum(
        "chqk,cqhd->ckhd", probs_b, d_mixed, preferred_element_type=jnp.float32
    ).astype(jnp.bfloat16)
    d_keys = d_keys.reshape(keys.shape)
    d_values = d_values.reshape(values.shape)
    key_term = jnp.einsum("cste,cstf->ef", slots, d_keys, preferred_element_type=jnp.float32)
    value_term = jnp.einsum("cste,cstf->ef", slots, d_values, preferred_element_type=jnp.float32)
    grad_wk, grad_wv = (
        lax.psum_scatter(
            key_term.astype(jnp.bfloat16), "db", scatter_dimension=0, tiled=True
        ).astype(jnp.float32),
        lax.psum_scatter(
            value_term.astype(jnp.bfloat16), "db", scatter_dimension=0, tiled=True
        ).astype(jnp.float32),
    )
    return (attended, grad_queries, grad_wk, grad_wv, grad_wo)


def solution(mesh):
    placed = (
        P("db", "head"),
        P(None, "head"),
        P(None, "head"),
        P("head", None),
        P("db", "head", None),
        P("db", None),
        P("db", None),
        P("db"),
        P("db", "head"),
    )
    return jax.shard_map(
        shards,
        mesh=mesh,
        in_specs=placed,
        out_specs=(
            P("db", "head"),
            P("db", "head"),
            P("db", "head"),
            P("db", "head"),
            P("head", "db"),
        ),
        check_vma=False,
    )
```

profile of v0, /device:TPU:0, one launch (start us, length us, event | category | flops | bytes accessed | tf_op | source)
XLA Modules:
  0.0 922.4 jit_solution(17145590493972607564)
XLA Ops:
  7.2 0.8 select_reduce_fusion
  7.9 0.1 copy.44
  8.0 15.4 %all_to_all.14 = s32[2,16,1]{0,2,1:T(1,128)S(1)} all-to-all(s32[2,16,1]{0,2,1:T(1,128)S(1)} %copy.44), channel_id=1, replica_groups=mesh['db'=16,'head'=2] {'db'}, dimensions={1} | all-to-all | bytes 256 | tf_op jit(solution)/shard_map/all_to_all | solution.py:24
  23.4 0.1 copy.45
  23.5 0.1 copy.46
  23.6 0.1 reshape.125
  23.7 5.8 gather_fusion
  29.6 2.5 broadcast_select_fusion
  32.0 3.8 copy.47
  35.8 6.9 broadcast_in_dim.50
  42.7 3.8 all-to-all-start.1
  46.5 0.7 all-gather.2.cloned.1.call-update
  47.2 0.5 reduce-scatter.9.cloned.1.call-start
  47.7 0.1 copy.73
  47.9 0.1 broadcast_compare_fusion
  48.0 11.1 %all-gather.2.cloned.1.call-done = bf16[128,4096]{1,0:T(8,128)(2,1)} async-done(((bf16[128,2048]{1,0:T(8,128)(2,1)}), bf16[128,4096]{1,0:T(8,128)(2,1)}) %all-gather.2.cloned.1.call-update) | async-done | bytes 1048592 | tf_op jit(solution)/shard_map/all_gather | solution.py:62
  59.1 11.8 %fusion.46 = bf16[16,8,16,128]{3,1,2,0:T(8,128)(2,1)S(1)} fusion(bf16[128,4096]{1,0:T(8,128)(2,1)} %all-gather.2.cloned.1.call-done, bf16[2048,4096]{1,0:T(8,128)(2,1)} %param.12), kind=kOutput, calls=%fused_computation.40 | convolution fusion | flops 2147745792 | bytes 18350080 | tf_op jit(solution)/shard_map/dot_general | solution.py:63
  70.9 0.1 copy.76
  71.0 138.6 %all-to-all-done.1 = bf16[2,2048,896]{2,0,1:T(2,128)(2,1)} async-done(((bf16[2,2048,896]{2,0,1:T(2,128)(2,1)}), bf16[2,2048,896]{2,0,1:T(2,128)(2,1)}, u32[]{:S(2)}, u32[]{:S(2)}) %all-to-all-start.1) | async-done | bytes 7340064 | tf_op jit(solution)/shard_map/all_to_all | solution.py:31
  209.6 11.4 %fusion.26 = bf16[2,8,128,896]{3,1,2,0:T(8,128)(2,1)S(1)} fusion(bf16[2,16,128,896]{3,0,2,1:T(2,128)(2,1)} %bitcast.6, s32[2,8]{1,0:T(2,128)S(1)} %copy-done.3), kind=kOutput, calls=%fused_computation.33 | convolution fusion | flops 60555520 | bytes 11010112 | tf_op jit(solution)/shard_map/ckn,cnte->ckte/dot_general | solution.py:33
  221.0 11.1 %convolution_convert_fusion.2 = bf16[2,8,128,2048]{3,2,1,0:T(8,128)(2,1)} fusion(bf16[896,2048]{1,0:T(8,128)(2,1)S(1)} %copy-done.5, bf16[2,8,128,896]{3,1,2,0:T(8,128)(2,1)S(1)} %fusion.26), kind=kOutput, calls=%fused_computation.25 | convolution fusion | flops 7520387072 | bytes 15728640 | tf_op jit(solution)/shard_map/cste,ef->cstf/dot_general | solution.py:36
  232.1 9.8 %copy.72 = bf16[256,8,16,128]{3,2,1,0:T(8,128)(2,1)} copy(bf16[256,8,16,128]{3,1,2,0:T(8,128)(2,1)} %bitcast.117) | data formatting | bytes 16777216
  241.9 13.2 %convolution_convert_fusion.3 = bf16[2,8,128,2048]{3,2,1,0:T(8,128)(2,1)} fusion(bf16[896,2048]{1,0:T(8,128)(2,1)} %param.11, bf16[2,8,128,896]{3,1,2,0:T(8,128)(2,1)S(1)} %fusion.26), kind=kOutput, calls=%fused_computation.26 | convolution fusion | flops 7520387072 | bytes 15728640 | tf_op jit(solution)/shard_map/cste,ef->cstf/dot_general | solution.py:39
  255.1 9.9 %copy.74 = bf16[256,8,16,128]{3,2,1,0:T(8,128)(2,1)} copy(bf16[256,8,16,128]{3,1,2,0:T(8,128)(2,1)} %bitcast.118) | data formatting | bytes 16777216
  265.0 11.8 %fusion.4 = f32[2,16,64,1024]{3,2,1,0:T(8,128)} fusion(bf16[2,1024,16,128]{3,2,1,0:T(8,128)(2,1)} %bitcast.107, bf16[2,64,16,128]{3,2,1,0:T(8,128)(2,1)S(1)} %bitcast.121), kind=kOutput, calls=%fused_computation.12 | convolution fusion | flops 536870912 | bytes 17301504 | tf_op jit(solution)/shard_map/cqhd,ckhd->chqk/dot_general | solution.py:75
  276.8 7.8 bitcast_reduce_fusion
  284.6 9.0 convolution_convert_fusion.1
  293.7 27.4 %convert_bitcast_fusion = bf16[2,1024,16,128]{3,1,2,0:T(8,128)(2,1)} fusion(f32[2,16,64,1024]{3,2,1,0:T(8,128)} %fusion.4, bf16[2,64,16,128]{3,2,1,0:T(8,128)(2,1)S(1)} %bitcast.127, f32[2,16,1024,64]{2,3,1,0:T(8,128)} %get-tuple-element.8, f32[2,16,64]{2,1,0:T(8,128)S(1)} %get-tuple-element.7, pred[2,1024]{1,0:T(4,128)(4,1)S(1)} %broadcast_compare_fusion), kind=kOutput, calls=%fused_computation.7 | convolution fusion | flops 564136960 | bytes 25700352 | tf_op jit(solution)/shard_map/chqk,cqhd->ckhd/dot_general | solution.py:84
  321.0 8.8 copy.78
  329.8 13.6 %copy.64 = bf16[2,8,128,2048]{3,1,2,0:T(8,128)(2,1)} copy(bf16[2,8,128,2048]{2,1,3,0:T(8,128)(2,1)} %bitcast.109) | data formatting | bytes 16777216 | tf_op jit(solution)/shard_map/reshape | solution.py:91
  343.4 12.9 %bitcast_convert_fusion = bf16[896,2048]{1,0:T(8,128)(2,1)} fusion(bf16[2,8,128,896]{3,1,2,0:T(8,128)(2,1)} %copy-done.1, bf16[2,8,128,2048]{3,1,2,0:T(8,128)(2,1)} %copy.64), kind=kOutput, calls=%fused_computation.20 | convolution fusion | flops 7518027776 | bytes 15728640 | tf_op jit(solution)/shard_map/cste,cstf->ef/dot_general | solution.py:93
  356.2 12.0 %copy.61 = bf16[2,1024,16,128]{3,2,1,0:T(8,128)(2,1)} copy(bf16[2,1024,16,128]{3,1,2,0:T(8,128)(2,1)} %convert_bitcast_fusion) | data formatting | bytes 16777216 | tf_op jit(solution)/shard_map/convert_element_type | solution.py:86
  368.2 13.3 %reshape.121 = bf16[2,8,128,2048]{3,2,1,0:T(8,128)(2,1)} reshape(bf16[2,1024,16,128]{3,2,1,0:T(8,128)(2,1)} %copy.61) | data formatting | bytes 16777216 | tf_op jit(solution)/shard_map/reshape | solution.py:90
  381.6 14.0 %bitcast_convert_fusion.1 = bf16[896,2048]{1,0:T(8,128)(2,1)} fusion(bf16[2,8,128,896]{3,1,2,0:T(8,128)(2,1)} %copy-done.1, bf16[2,8,128,2048]{3,2,1,0:T(8,128)(2,1)} %reshape.121), kind=kOutput, calls=%fused_computation.21 | convolution fusion | flops 7518027776 | bytes 15728640 | tf_op jit(solution)/shard_map/cste,cstf->ef/dot_general | solution.py:92
  395.6 10.8 %fusion.47 = bf16[2,64,16,128]{3,1,2,0:T(8,128)(2,1)S(1)} fusion(bf16[2,1024,16,128]{3,2,1,0:T(8,128)(2,1)} %bitcast.108, f32[2,16,1024,64]{2,3,1,0:T(8,128)} %get-tuple-element.8, f32[2,16,64]{2,1,0:T(8,128)S(1)} %get-tuple-element.7, pred[2,1024]{1,0:T(4,128)(4,1)S(1)} %broadcast_compare_fusion), kind=kOutput, calls=%fused_computation.41 | convolution fusion | flops 545521664 | bytes 17311744 | tf_op jit(solution)/shard_map/chqk,ckhd->cqhd/dot_general | solution.py:56
  406.4 0.3 copy.55
  406.8 8.5 convolution_convert_fusion
  415.3 9.2 %convolution_convert_fusion.4 = bf16[128,4096]{1,0:T(8,128)(2,1)} fusion(bf16[2048,4096]{1,0:T(8,128)(2,1)} %param.12, bf16[16,8,16,128]{3,2,1,0:T(8,128)(2,1)S(1)} %bitcast.120), kind=kOutput, calls=%fused_computation.27 | convolution fusion | flops 2148007936 | bytes 18350080 | tf_op jit(solution)/shard_map/dot_general | solution.py:58
  424.6 23.7 %fusion.41 = bf16[2,64,16,128]{3,1,2,0:T(8,128)(2,1)S(1)} fusion(bf16[2,1024,16,128]{3,2,1,0:T(8,128)(2,1)} %bitcast.112, f32[2,16,64,1024]{3,2,1,0:T(8,128)} %fusion.4, f32[2,16,1024,64]{2,3,1,0:T(8,128)} %get-tuple-element.8, f32[2,16,64]{2,1,0:T(8,128)S(1)} %get-tuple-element.7, pred[2,1024]{1,0:T(4,128)(4,1)S(1)} %broadcast_compare_fusion), kind=kOutput, calls=%fused_computation.39 | convolution fusion | flops 560204800 | bytes 25700352 | tf_op jit(solution)/shard_map/chqk,ckhd->cqhd/dot_general | solution.py:80
  448.3 0.3 copy.59
  448.7 0.9 copy.128
  449.6 15.2 %reduce-scatter.9.cloned.1.call-done = bf16[56,2048]{1,0:T(8,128)(2,1)} async-done(((bf16[896,2048]{1,0:T(8,128)(2,1)}), bf16[56,2048]{1,0:T(8,128)(2,1)}) %reduce-scatter.9.cloned.1.call-update) | async-done | bytes 229392 | tf_op jit(solution)/shard_map/reduce_scatter | solution.py:98
  464.8 1.7 convert_element_type.82
  466.6 85.0 %reduce-scatter.7.cloned.1.call-done = bf16[56,2048]{1,0:T(8,128)(2,1)} async-done(((bf16[896,2048]{1,0:T(8,128)(2,1)}), bf16[56,2048]{1,0:T(8,128)(2,1)}) %reduce-scatter.7.cloned.1.call-update) | async-done | bytes 229392 | tf_op jit(solution)/shard_map/reduce_scatter | solution.py:95
  551.6 1.7 convert_element_type.78
  553.3 345.2 %reduce-scatter.11.cloned.1.call-done = bf16[2048,256]{1,0:T(8,128)(2,1)} async-done(((bf16[2048,4096]{1,0:T(8,128)(2,1)}), bf16[2048,256]{1,0:T(8,128)(2,1)}) %reduce-scatter.11.cloned.1.call-update) | async-done | bytes 1048592 | tf_op jit(solution)/shard_map/reduce_scatter | solution.py:71
  898.6 2.7 convert_element_type.84
  901.3 14.2 %reduce-scatter.5.cloned.1.call-done = bf16[128,2048]{1,0:T(8,128)(2,1)} async-done(((bf16[128,4096]{1,0:T(8,128)(2,1)}), bf16[128,2048]{1,0:T(8,128)(2,1)}) %reduce-scatter.5.cloned.1.call-update) | async-done | bytes 524304 | tf_op jit(solution)/shard_map/reduce_scatter | solution.py:59
  (28 shorter events, 0.3 us)
Async XLA Ops:
  42.7 5.0 copy-start.2
  42.7 5.2 copy-start.4
  42.7 166.9 %all-to-all-start.1 = ((bf16[2,2048,896]{2,0,1:T(2,128)(2,1)}), bf16[2,2048,896]{2,0,1:T(2,128)(2,1)}, u32[]{:S(2)}, u32[]{:S(2)}) async-start(bf16[2,2048,896]{2,0,1:T(2,128)(2,1)} %bitcast.110), calls=%async_computation.1 | async-start | bytes 14680064 | tf_op jit(solution)/shard_map/all_to_all | solution.py:31
  46.5 12.6 %all-gather.2.cloned.1.call-start = ((), (), s32[]{:S(2)}) async-start(), calls=%async_computation.7 | async-start | bytes 1572864 | tf_op jit(solution)/shard_map/all_gather | solution.py:62
  47.2 417.6 %reduce-scatter.9.cloned.1.call-start = ((), (), s32[]{:S(2)}) async-start(), calls=%async_computation.9 | async-start | bytes 3899392 | tf_op jit(solution)/shard_map/reduce_scatter | solution.py:98
  47.9 161.7 %copy-start.3 = (s32[2,8]{1,0:T(2,128)S(1)}, s32[2,8]{1,0:T(2,128)}, u32[]{:S(2)}) copy-start(s32[2,8]{1,0:T(2,128)} %param.15) | copy-start | bytes 196
  209.6 11.4 %copy-start.5 = (bf16[896,2048]{1,0:T(8,128)(2,1)S(1)}, bf16[896,2048]{1,0:T(8,128)(2,1)}, u32[]{:S(2)}) copy-start(bf16[896,2048]{1,0:T(8,128)(2,1)} %param.10) | copy-start | bytes 11010052
  221.0 20.9 %copy-start.1 = (bf16[2,8,128,896]{3,1,2,0:T(8,128)(2,1)}, bf16[2,8,128,896]{3,1,2,0:T(8,128)(2,1)S(1)}, u32[]{:S(2)}) copy-start(bf16[2,8,128,896]{3,1,2,0:T(8,128)(2,1)S(1)} %fusion.26) | copy-start | bytes 11010052
  255.1 21.7 %slice-start = ((s8[8388608]{0:T(1024)(128)(4,1)}), s8[4194304]{0:T(1024)(128)(4,1)S(1)}, s32[]{:S(2)}) async-start(s8[8388608]{0:T(1024)(128)(4,1)} %bitcast.113), calls=%async_computation.11 | async-start | bytes 8388608
  265.0 11.8 %slice-start.1 = ((s8[8388608]{0:T(1024)(128)(4,1)}), s8[4194304]{0:T(1024)(128)(4,1)S(1)}, s32[]{:S(2)}) async-start(s8[8388608]{0:T(1024)(128)(4,1)} %bitcast.113), calls=%async_computation.12 | async-start | bytes 8388608
  381.5 170.1 %reduce-scatter.7.cloned.1.call-start = ((), (), s32[]{:S(2)}) async-start(), calls=%async_computation.8 | async-start | bytes 3899392 | tf_op jit(solution)/shard_map/reduce_scatter | solution.py:95
  395.6 11.2 %copy-start = (bf16[128,4096]{1,0:T(8,128)(2,1)S(1)}, bf16[128,4096]{1,0:T(8,128)(2,1)}, u32[]{:S(2)}) copy-start(bf16[128,4096]{1,0:T(8,128)(2,1)} %all-gather.2.cloned.1.call-done) | copy-start | bytes 3145732
  395.6 503.0 %reduce-scatter.11.cloned.1.call-start = ((), (), s32[]{:S(2)}) async-start(), calls=%async_computation.10 | async-start | bytes 17825792 | tf_op jit(solution)/shard_map/reduce_scatter | solution.py:71
  415.3 500.1 %reduce-scatter.5.cloned.1.call-start = ((), (), s32[]{:S(2)}) async-start(), calls=%async_computation.6 | async-start | bytes 1572864 | tf_op jit(solution)/shard_map/reduce_scatter | solution.py:59
Sparse Core Ops, SparseCore 0:
  48.9 10.1 all-gather.1
  381.6 83.1 reduce-scatter.8
  467.2 84.3 reduce-scatter.6
  553.8 344.7 reduce-scatter.10
  901.3 14.1 reduce-scatter.4
where the time goes:
time: 928 us; the launch traced here: 922 us
  waiting for transfers between devices  610 us (66%)
  matrix products  183 us (20%)
  local copies, waits for them, and re-layouts  86 us (9%)
  blocking collectives  15.4 us (2%)
  between operations  14.4 us (2%)
  other arithmetic  9.53 us (1%)
    reduce_scatter x1, waiting for transfers between devices, shards(): lax.psum_scatter(out_grad.astype(jnp.bfloat16), 'db', scatter_dimension=1...  345 us
    all_to_all x1, waiting for transfers between devices, shards(): lax.all_to_all(spread, ('db', 'head'), split_axis=1, concat_axis=1, tiled...  139 us
    reduce_scatter x1, waiting for transfers between devices, shards(): lax.psum_scatter(key_term.astype(jnp.bfloat16), 'db', scatter_dimension=0...  85 us
    unnamed x22, local copies, waits for them, and re-layouts  29.6 us
    dot_general x1, matrix products, shards(): jnp.einsum('chqk,cqhd->ckhd', d_scores, query_heads, preferred_element_ty...  27.4 us
    dot_general x1, matrix products, shards(): jnp.einsum('chqk,ckhd->cqhd', d_scores, key_heads, preferred_element_type...  23.7 us
  transfers between devices with their start and end apart: 6, of which 6 were waited for; matrix products, arithmetic and copies ran while one was open for 9% of the time, Pallas kernels for 0%

commit v1 on v0

v1 whole, which is shorter than its diff:
```python
import functools
import math

import jax
import jax.numpy as jnp
from jax import lax
from jax.experimental import pallas as pl
from jax.experimental.pallas import tpu as pltpu
from jax.sharding import PartitionSpec as P

HD = 128
F32 = jnp.float32
BF16 = jnp.bfloat16
VMEM_LIMIT = 56 * 1024 * 1024


def nt(a, b):
    return lax.dot_general(a, b, (((1,), (1,)), ((), ())), preferred_element_type=F32)


def nn(a, b):
    return jnp.dot(a, b, preferred_element_type=F32)


def tn(a, b):
    return lax.dot_general(a, b, (((0,), (0,)), ((), ())), preferred_element_type=F32)


def forward_kernel(groups, heads, count_ref, slots_ref, q_ref, dm_ref, wk_ref, wv_ref,
                   mixed_ref, probs_ref, gwv_ref, pulled_ref):
    tokens = q_ref.shape[0] // groups
    key_len = slots_ref.shape[1]
    tokens_per_slot = key_len // 8
    factor = 1.0 / math.sqrt(HD)
    for c in range(groups):
        rows = slice(c * tokens, (c + 1) * tokens)
        slots = slots_ref[c]
        lifted = jnp.concatenate(
            [
                nt(q_ref[rows, h * HD:(h + 1) * HD], wk_ref[:, h * HD:(h + 1) * HD]).astype(BF16)
                for h in range(heads)
            ],
            axis=0,
        )
        scores = nt(lifted, slots) * factor
        position = lax.broadcasted_iota(jnp.int32, (1, key_len), 1)
        live = position < count_ref[c] * tokens_per_slot
        expo = jnp.where(live, jnp.exp(scores), 0.0)
        probs = (expo / jnp.sum(expo, axis=-1, keepdims=True)).astype(BF16)
        probs_ref[0, c] = probs
        pulled = nn(probs, slots).astype(BF16)
        for h in range(heads):
            part = pulled[h * tokens:(h + 1) * tokens]
            cols = slice(h * HD, (h + 1) * HD)
            mixed_ref[rows, cols] = nn(part, wv_ref[:, cols]).astype(BF16)
            pulled_ref[h, rows, :] = part
    for h in range(heads):
        cols = slice(h * HD, (h + 1) * HD)
        gwv_ref[:, cols] = tn(pulled_ref[h], dm_ref[:, cols]).astype(BF16)


def backward_kernel(groups, heads, slots_ref, q_ref, dm_ref, wk_ref, wv_ref, probs_ref,
                    gq_ref, gwk_ref, pulled_ref):
    tokens = q_ref.shape[0] // groups
    factor = 1.0 / math.sqrt(HD)
    for c in range(groups):
        rows = slice(c * tokens, (c + 1) * tokens)
        slots = slots_ref[c]
        lifted = jnp.concatenate(
            [
                nt(dm_ref[rows, h * HD:(h + 1) * HD], wv_ref[:, h * HD:(h + 1) * HD]).astype(BF16)
                for h in range(heads)
            ],
            axis=0,
        )
        d_probs = nt(lifted, slots)
        probs = probs_ref[0, c].astype(F32)
        weighted = probs * d_probs
        inner = jnp.sum(weighted, axis=-1, keepdims=True)
        d_scores = ((weighted - probs * inner) * factor).astype(BF16)
        pulled = nn(d_scores, slots).astype(BF16)
        for h in range(heads):
            part = pulled[h * tokens:(h + 1) * tokens]
            cols = slice(h * HD, (h + 1) * HD)
            gq_ref[rows, cols] = nn(part, wk_ref[:, cols]).astype(BF16)
            pulled_ref[h, rows, :] = part
    for h in range(heads):
        cols = slice(h * HD, (h + 1) * HD)
        gwk_ref[:, cols] = tn(pulled_ref[h], q_ref[:, cols]).astype(BF16)


def attention_calls(slots, queries, d_mixed, w_key, w_value, nbr_count):
    groups, key_len, enc = slots.shape
    tok_rows, width = queries.shape
    heads = min(4, width // HD)
    steps = width // (heads * HD)
    part = heads * HD
    group_rows = heads * (tok_rows // groups)
    whole = pl.BlockSpec((groups, key_len, enc), lambda i: (0, 0, 0))
    tok = pl.BlockSpec((tok_rows, part), lambda i: (0, i))
    weight = pl.BlockSpec((enc, part), lambda i: (0, i))
    prob = pl.BlockSpec((1, groups, group_rows, key_len), lambda i: (i, 0, 0, 0))
    tok_shape = jax.ShapeDtypeStruct((tok_rows, width), BF16)
    weight_shape = jax.ShapeDtypeStruct((enc, width), BF16)
    prob_shape = jax.ShapeDtypeStruct((steps, groups, group_rows, key_len), BF16)
    cost = pl.CostEstimate(
        flops=int(4 * groups * group_rows * key_len * enc * steps * 1.2),
        bytes_accessed=20_000_000,
        transcendentals=groups * group_rows * steps * key_len,
    )
    common = dict(
        grid=(steps,),
        scratch_shapes=[pltpu.VMEM((heads, tok_rows, enc), BF16)],
        compiler_params=pltpu.CompilerParams(vmem_limit_bytes=VMEM_LIMIT),
        cost_estimate=cost,
    )
    mixed, probs, gwv = pl.pallas_call(
        functools.partial(forward_kernel, groups, heads),
        in_specs=[pl.BlockSpec(memory_space=pltpu.SMEM), whole, tok, tok, weight, weight],
        out_specs=[tok, prob, weight],
        out_shape=[tok_shape, prob_shape, weight_shape],
        **common,
    )(nbr_count, slots, queries, d_mixed, w_key, w_value)
    gq, gwk = pl.pallas_call(
        functools.partial(backward_kernel, groups, heads),
        in_specs=[whole, tok, tok, weight, weight, prob],
        out_specs=[tok, weight],
        out_shape=[tok_shape, weight_shape],
        **common,
    )(slots, queries, d_mixed, w_key, w_value, probs)
    return mixed, gwv, gq, gwk


def shards(queries, w_key, w_value, w_out, encodings, nbr_row, nbr_owner, nbr_count, grad_out):
    db_count = lax.axis_size("db")
    head_count = lax.axis_size("head")
    groups, slot_count = nbr_row.shape
    tok_rows, local_width = queries.shape
    enc_width = encodings.shape[2]
    slice_len = encodings.shape[1]
    owner_ids = lax.broadcasted_iota(jnp.int32, (1, 1, db_count), 2)
    chosen = nbr_owner[:, :, None] == owner_ids
    wanted = jnp.sum(jnp.where(chosen, nbr_row[:, :, None], 0), axis=1)
    incoming = lax.all_to_all(wanted, "db", split_axis=1, concat_axis=1, tiled=True)
    table = jnp.take(encodings, incoming.T.reshape(-1), axis=0, mode="clip")
    table = table.reshape(db_count, groups * slice_len, enc_width)
    received = lax.all_to_all(table, "db", split_axis=0, concat_axis=0, tiled=True)
    received = received.reshape(db_count * groups, slice_len, enc_width)
    piece = lax.all_gather(grad_out, "head", axis=1, tiled=True)
    d_mixed = lax.dot_general(
        piece, w_out, (((1,), (1,)), ((), ())), preferred_element_type=F32
    ).astype(BF16)
    out_cols = lax.all_to_all(piece, "db", split_axis=1, concat_axis=0, tiled=True)
    picks = nbr_owner * groups + lax.broadcasted_iota(jnp.int32, nbr_owner.shape, 0)
    mine = jnp.take(received, picks.reshape(-1), axis=0, mode="clip")
    slots = lax.all_gather(mine, "head", axis=1, tiled=True)
    slots = slots.reshape(groups, slot_count * slice_len * head_count, enc_width)
    mixed, gwv, gq, gwk = attention_calls(slots, queries, d_mixed, w_key, w_value, nbr_count)
    mixed_all = lax.all_gather(mixed, "db", axis=0, tiled=True)
    out_term = jnp.dot(mixed, w_out, preferred_element_type=F32)
    attended = lax.psum_scatter(out_term.astype(BF16), "head", scatter_dimension=1, tiled=True)
    grad_wo = lax.dot_general(
        mixed_all, out_cols, (((0,), (0,)), ((), ())), preferred_element_type=F32
    )
    grad_wv = lax.psum_scatter(gwv, "db", scatter_dimension=0, tiled=True).astype(F32)
    grad_wk = lax.psum_scatter(gwk, "db", scatter_dimension=0, tiled=True).astype(F32)
    return (attended, gq, grad_wk, grad_wv, grad_wo)


def solution(mesh):
    placed = (
        P("db", "head"),
        P(None, "head"),
        P(None, "head"),
        P("head", None),
        P("db", "head", None),
        P("db", None),
        P("db", None),
        P("db"),
        P("db", "head"),
    )
    return jax.shard_map(
        shards,
        mesh=mesh,
        in_specs=placed,
        out_specs=(
            P("db", "head"),
            P("db", "head"),
            P("db", "head"),
            P("db", "head"),
            P("head", "db"),
        ),
        check_vma=False,
    )
```

time: 928 us -> 471 us (0.51)
  waiting for transfers between devices: 610 us -> 342 us
  matrix products: 183 us -> 29 us
  local copies, waits for them, and re-layouts: 86 us -> 11.9 us
  Pallas kernels: 0 us -> 41.9 us
    reduce_scatter x4 -> x3, waiting for transfers between devices: 460 us -> 126 us  [the longest x1 84.9 us: shards(): lax.psum_scatter(gwk, 'db', scatter_dimension=0, tiled=True).astype(F32)]
    dot_general x13 -> x2, matrix products: 171 us -> 16.4 us  [the longest x1 9.19 us: shards(): out_term = jnp.dot(mixed, w_out, preferred_element_type=F32)]
    all_gather x0 -> x2, waiting for transfers between devices: none -> 124 us  [the longest x1 113 us: shards(): mixed_all = lax.all_gather(mixed, 'db', axis=0, tiled=True)]
    all_to_all x1 -> x2, waiting for transfers between devices: 139 us -> 91 us  [the longest x1 68.3 us: shards(): lax.all_to_all(table, 'db', split_axis=0, concat_axis=0, tiled=True)]
    pallas_call x0 -> x2, Pallas kernels: none -> 41.9 us  [the longest x1 21.1 us: attention_calls(): pl.pallas_call(functools.partial(backward_kernel, groups, heads), in_spec...]
    unnamed x22 -> x7, local copies, waits for them, and re-layouts: 29.6 us -> 1.01 us
    reshape x2 -> x0, local copies, waits for them, and re-layouts: 26.9 us -> none  [the longest x1 13.6 us: shards(): d_values = d_values.reshape(values.shape)]
    convert_element_type x3 -> x0, local copies, waits for them, and re-layouts: 12.7 us -> none  [the longest x1 12 us: shards(): d_keys = jnp.einsum('chqk,cqhd->ckhd', d_scores, query_heads, preferred_e...]
  transfers between devices with their start and end apart: 6 -> 8, of which waited for: 6 -> 7; matrix products, arithmetic and copies ran while one was open for 9% -> 8% of each run, Pallas kernels for 0% -> 4%
where the time goes in v1:
time: 471 us; the launch traced here: 470 us
  waiting for transfers between devices  342 us (73%)
  Pallas kernels  41.9 us (9%)
  matrix products  29 us (6%)
  blocking collectives  15.4 us (3%)
  between operations  14.2 us (3%)
  local copies, waits for them, and re-layouts  11.9 us (3%)
  starting transfers between devices  11.9 us (3%)
    all_gather x1, waiting for transfers between devices, shards(): mixed_all = lax.all_gather(mixed, 'db', axis=0, tiled=True)  113 us
    reduce_scatter x1, waiting for transfers between devices, shards(): lax.psum_scatter(gwk, 'db', scatter_dimension=0, tiled=True).astype(F32)  84.9 us
    all_to_all x1, waiting for transfers between devices, shards(): lax.all_to_all(table, 'db', split_axis=0, concat_axis=0, tiled=True)  68.3 us
    reduce_scatter x1, waiting for transfers between devices, shards(): lax.psum_scatter(gwv, 'db', scatter_dimension=0, tiled=True).astype(F32)  39.3 us
    all_to_all x1, waiting for transfers between devices, shards(): lax.all_to_all(piece, 'db', split_axis=1, concat_axis=0, tiled=True)  22.8 us
    pallas_call x1, Pallas kernels, attention_calls(): pl.pallas_call(functools.partial(backward_kernel, groups, heads), in_spec...  21.1 us
    pallas_call x1, Pallas kernels, attention_calls(): pl.pallas_call(functools.partial(forward_kernel, groups, heads), in_specs...  20.7 us
    all_to_all x1, blocking collectives, shards(): lax.all_to_all(wanted, 'db', split_axis=1, concat_axis=1, tiled=True)  15.4 us
  transfers between devices with their start and end apart: 8, of which 7 were waited for; matrix products, arithmetic and copies ran while one was open for 8% of the time, Pallas kernels for 4%

profile of v1, /device:TPU:0, one launch (start us, length us, event | category | flops | bytes accessed | tf_op | source)
XLA Modules:
  0.0 470.1 jit_solution(11786519244795799768)
XLA Ops:
  7.2 0.8 select_reduce_fusion
  7.9 0.1 copy.24
  8.0 15.4 %all_to_all.36 = s32[2,16,1]{0,2,1:T(1,128)S(1)} all-to-all(s32[2,16,1]{0,2,1:T(1,128)S(1)} %copy.24), channel_id=1, replica_groups=mesh['db'=16,'head'=2] {'db'}, dimensions={1} | all-to-all | bytes 256 | tf_op jit(solution)/shard_map/all_to_all | solution.py:144
  23.4 0.1 copy.25
  23.5 0.1 copy.26
  23.6 0.1 reshape.35
  23.7 5.9 %gather_fusion = bf16[32,64,896]{2,1,0:T(8,128)(2,1)} fusion(bf16[64,64,896]{2,1,0:T(8,128)(2,1)} %param.13, s32[1024]{0:T(1024)S(1)} %pad_clamp_fusion.1), kind=kCustom, calls=%fused_computation | custom fusion | bytes 7340160 | tf_op jit(solution)/shard_map/jit(_take)/gather | solution.py:145
  29.6 0.0 copy-start.1
  29.6 0.0 copy-start.2
  29.6 4.6 all-to-all-start.1
  34.2 0.0 all-gather.5.cloned.1.call-start
  34.3 0.0 copy-done.1
  34.3 1.0 copy.27
  35.3 0.0 all-gather.5.cloned.1.call-update
  35.3 0.0 all-gather.9.cloned.1.call-start
  35.4 0.0 copy-done.2
  35.4 0.1 reshape.43
  35.5 68.3 %all-to-all-done.1 = bf16[16,128,896]{2,1,0:T(8,128)(2,1)} async-done(((bf16[16,128,896]{2,1,0:T(8,128)(2,1)}), bf16[16,128,896]{2,1,0:T(8,128)(2,1)}, u32[]{:S(2)}, u32[]{:S(2)}) %all-to-all-start.1) | async-done | bytes 3670048 | tf_op jit(solution)/shard_map/all_to_all | solution.py:147
  103.8 4.0 gather_fusion.1
  107.8 0.0 all-gather.9.cloned.1.call-update
  107.8 0.0 reduce-scatter.8.cloned.1.call-start
  107.9 0.0 all-gather.5.cloned.1.call-done
  107.9 12.6 %convolution_convert_fusion.1.dm_ref = bf16[128,2048]{1,0:T(8,128)(2,1)} fusion(bf16[128,4096]{0,1:T(8,128)(2,1)} %all-gather.5.cloned.1.call-done, bf16[2048,4096]{1,0:T(8,128)(2,1)} %param.12), kind=kOutput, calls=%fused_computation.3 | convolution fusion | flops 2147745792 | bytes 18350080 | tf_op jit(solution)/shard_map/dot_general | solution.py:150
  120.5 10.7 %all-gather.9.cloned.1.call-done = bf16[16,128,896]{2,1,0:T(8,128)(2,1)} async-done(((bf16[16,64,896]{2,1,0:T(8,128)(2,1)}), bf16[16,128,896]{2,1,0:T(8,128)(2,1)}) %all-gather.9.cloned.1.call-update) | async-done | bytes 3670032 | tf_op jit(solution)/shard_map/all_gather | solution.py:156
  131.2 20.7 %shard_map.128 = (bf16[128,2048]{1,0:T(8,128)(2,1)}, bf16[4,2,256,1024]{3,2,1,0:T(8,128)(2,1)}, bf16[896,2048]{1,0:T(8,128)(2,1)}) custom-call(s32[2]{0:T(128)} %count_ref.1, bf16[2,1024,896]{2,1,0:T(8,128)(2,1)} %bitcast.21, bf16[128,2048]{1,0:T(8,128)(2,1)} %q_ref.3, bf16[128,2048]{1,0:T(8,128)(2,1)} %convolution_convert_fusion.1.dm_ref, ...), custom_call_target="tpu_custom_call" | custom-call | flops 9019430912 | bytes 20000000 | tf_op jit(solution)/shard_map/pallas_call | solution.py:117
  152.0 0.0 reduce-scatter.8.cloned.1.call-update
  152.0 0.2 reduce-scatter.6.cloned.1.call-start
  152.2 21.1 %shard_map.129 = (bf16[128,2048]{1,0:T(8,128)(2,1)}, bf16[896,2048]{1,0:T(8,128)(2,1)}) custom-call(bf16[2,1024,896]{2,1,0:T(8,128)(2,1)} %bitcast.22, bf16[128,2048]{1,0:T(8,128)(2,1)} %q_ref.3, bf16[128,2048]{1,0:T(8,128)(2,1)} %convolution_convert_fusion.1.dm_ref, bf16[896,2048]{1,0:T(8,128)(2,1)} %wk_ref.3, bf16[896,2048]{1,0:T(8,128)(2,1)} %wv_ref.3, ...), custom_call_target="tpu_custom_call" | custom-call | flops 9019430912 | bytes 20000000 | tf_op jit(solution)/shard_map/pallas_call | solution.py:124
  173.4 0.0 copy-start
  173.4 0.0 reduce-scatter.6.cloned.1.call-update
  173.4 0.0 all-gather.7.cloned.1.call-start
  173.4 0.5 all-gather.7.cloned.1.call-update
  174.0 6.8 %all-to-all-start.2 = ((bf16[128,16,256]{0,2,1:T(8,128)(2,1)}), bf16[128,16,256]{0,2,1:T(8,128)(2,1)S(1)}, u32[]{:S(2)}, u32[]{:S(2)}) async-start(bf16[128,16,256]{0,2,1:T(8,128)(2,1)} %bitcast.6), calls=%async_computation.5 | async-start | bytes 2097152 | tf_op jit(solution)/shard_map/all_to_all | solution.py:153
  180.8 0.0 reduce-scatter.4.cloned.1.call-start
  180.8 0.0 copy-done
  180.8 9.2 %convolution_convert_fusion = bf16[128,4096]{1,0:T(8,128)(2,1)} fusion(bf16[128,2048]{1,0:T(8,128)(2,1)S(1)} %copy-done, bf16[2048,4096]{1,0:T(8,128)(2,1)} %param.12), kind=kOutput, calls=%fused_computation.2 | convolution fusion | flops 2148007936 | bytes 18350080 | tf_op jit(solution)/shard_map/dot_general | solution.py:160
  190.0 0.0 reduce-scatter.4.cloned.1.call-update
  190.1 22.8 %all-to-all-done.2 = bf16[128,16,256]{0,2,1:T(8,128)(2,1)S(1)} async-done(((bf16[128,16,256]{0,2,1:T(8,128)(2,1)}), bf16[128,16,256]{0,2,1:T(8,128)(2,1)S(1)}, u32[]{:S(2)}, u32[]{:S(2)}) %all-to-all-start.2) | async-done | bytes 1048608 | tf_op jit(solution)/shard_map/all_to_all | solution.py:153
  212.8 0.5 copy.28
  213.3 39.3 %reduce-scatter.8.cloned.1.call-done = bf16[56,2048]{1,0:T(8,128)(2,1)} async-done(((bf16[896,2048]{1,0:T(8,128)(2,1)}), bf16[56,2048]{1,0:T(8,128)(2,1)}) %reduce-scatter.8.cloned.1.call-update) | async-done | bytes 229392 | tf_op jit(solution)/shard_map/reduce_scatter | solution.py:165
  252.6 1.7 convert_element_type.15
  254.3 84.9 %reduce-scatter.6.cloned.1.call-done = bf16[56,2048]{1,0:T(8,128)(2,1)} async-done(((bf16[896,2048]{1,0:T(8,128)(2,1)}), bf16[56,2048]{1,0:T(8,128)(2,1)}) %reduce-scatter.6.cloned.1.call-update) | async-done | bytes 229392 | tf_op jit(solution)/shard_map/reduce_scatter | solution.py:166
  339.2 1.7 convert_element_type.14
  341.0 112.8 %all-gather.7.cloned.1.call-done = bf16[2048,2048]{1,0:T(8,128)(2,1)} async-done(((bf16[128,2048]{1,0:T(8,128)(2,1)}), bf16[2048,2048]{1,0:T(8,128)(2,1)}) %all-gather.7.cloned.1.call-update) | async-done | bytes 8388624 | tf_op jit(solution)/shard_map/all_gather | solution.py:159
  453.8 7.2 %fusion = f32[2048,256]{1,0:T(8,128)} fusion(bf16[2048,2048]{1,0:T(8,128)(2,1)} %all-gather.7.cloned.1.call-done, bf16[2048,256]{1,0:T(8,128)(2,1)S(1)} %bitcast.18), kind=kOutput, calls=%fused_computation.9 | convolution fusion | flops 2147483648 | bytes 11534336 | tf_op jit(solution)/shard_map/dot_general | solution.py:162
  461.0 2.3 reduce-scatter.4.cloned.1.call-done
  (3 shorter events, 0.0 us)
Async XLA Ops:
  29.6 4.7 copy-start.1
  29.6 5.8 %copy-start.2 = (s32[2,8]{1,0:T(2,128)S(1)}, s32[2,8]{1,0:T(2,128)}, u32[]{:S(2)}) copy-start(s32[2,8]{1,0:T(2,128)} %param.15) | copy-start | bytes 196
  29.6 74.2 %all-to-all-start.1 = ((bf16[16,128,896]{2,1,0:T(8,128)(2,1)}), bf16[16,128,896]{2,1,0:T(8,128)(2,1)}, u32[]{:S(2)}, u32[]{:S(2)}) async-start(bf16[16,128,896]{2,1,0:T(8,128)(2,1)} %bitcast.16), calls=%async_computation.1 | async-start | bytes 7340032 | tf_op jit(solution)/shard_map/all_to_all | solution.py:147
  34.2 73.7 %all-gather.5.cloned.1.call-start = ((), (), s32[]{:S(2)}) async-start(), calls=%async_computation.6 | async-start | bytes 1572864 | tf_op jit(solution)/shard_map/all_gather | solution.py:149
  35.3 95.9 %all-gather.9.cloned.1.call-start = ((), (), s32[]{:S(2)}) async-start(), calls=%async_computation.11 | async-start | bytes 5505024 | tf_op jit(solution)/shard_map/all_gather | solution.py:156
  107.8 144.8 %reduce-scatter.8.cloned.1.call-start = ((), (), s32[]{:S(2)}) async-start(), calls=%async_computation.9 | async-start | bytes 3899392 | tf_op jit(solution)/shard_map/reduce_scatter | solution.py:165
  152.0 187.2 %reduce-scatter.6.cloned.1.call-start = ((), (), s32[]{:S(2)}) async-start(), calls=%async_computation.8 | async-start | bytes 3899392 | tf_op jit(solution)/shard_map/reduce_scatter | solution.py:166
  173.4 7.5 %copy-start = (bf16[128,2048]{1,0:T(8,128)(2,1)S(1)}, bf16[128,2048]{1,0:T(8,128)(2,1)}, u32[]{:S(2)}) copy-start(bf16[128,2048]{1,0:T(8,128)(2,1)} %get-tuple-element.10) | copy-start | bytes 1572868
  173.4 280.4 %all-gather.7.cloned.1.call-start = ((), (), s32[]{:S(2)}) async-start(), calls=%async_computation.10 | async-start | bytes 8912896 | tf_op jit(solution)/shard_map/all_gather | solution.py:159
  174.0 38.8 %all-to-all-start.2 = ((bf16[128,16,256]{0,2,1:T(8,128)(2,1)}), bf16[128,16,256]{0,2,1:T(8,128)(2,1)S(1)}, u32[]{:S(2)}, u32[]{:S(2)}) async-start(bf16[128,16,256]{0,2,1:T(8,128)(2,1)} %bitcast.6), calls=%async_computation.5 | async-start | bytes 2097152 | tf_op jit(solution)/shard_map/all_to_all | solution.py:153
  180.8 282.5 %reduce-scatter.4.cloned.1.call-start = ((), (), s32[]{:S(2)}) async-start(), calls=%async_computation.7 | async-start | bytes 1572864 | tf_op jit(solution)/shard_map/reduce_scatter | solution.py:161
Sparse Core Ops, SparseCore 0:
  37.2 10.2 all-gather.4
  107.9 23.2 all-gather.8
  152.1 100.4 reduce-scatter.7
  254.8 84.4 reduce-scatter.5
  342.4 111.3 all-gather.6
  456.5 6.7 reduce-scatter.3

commit v2 on v1

--- a/solution.py
+++ b/solution.py
@@ -1,4 +1,5 @@
 import functools
+import itertools
 import math
 
 import jax
@@ -26,8 +27,8 @@
     return lax.dot_general(a, b, (((0,), (0,)), ((), ())), preferred_element_type=F32)
 
 
-def forward_kernel(groups, heads, count_ref, slots_ref, q_ref, dm_ref, wk_ref, wv_ref,
-                   mixed_ref, probs_ref, gwv_ref, pulled_ref):
+def forward_kernel(groups, heads, count_ref, slots_ref, q_ref, wk_ref, wv_ref,
+                   mixed_ref, probs_ref, pulled_ref):
     tokens = q_ref.shape[0] // groups
     key_len = slots_ref.shape[1]
     tokens_per_slot = key_len // 8
@@ -54,13 +55,10 @@
             cols = slice(h * HD, (h + 1) * HD)
             mixed_ref[rows, cols] = nn(part, wv_ref[:, cols]).astype(BF16)
             pulled_ref[h, rows, :] = part
-    for h in range(heads):
-        cols = slice(h * HD, (h + 1) * HD)
-        gwv_ref[:, cols] = tn(pulled_ref[h], dm_ref[:, cols]).astype(BF16)
-
-
-def backward_kernel(groups, heads, slots_ref, q_ref, dm_ref, wk_ref, wv_ref, probs_ref,
-                    gq_ref, gwk_ref, pulled_ref):
+
+
+def backward_kernel(groups, heads, shares, slots_ref, q_ref, dm_ref, wk_ref, wv_ref, probs_ref,
+                    mixing_ref, gq_ref, gwkv_ref, pulled_ref):
     tokens = q_ref.shape[0] // groups
     factor = 1.0 / math.sqrt(HD)
     for c in range(groups):
@@ -86,49 +84,243 @@
             pulled_ref[h, rows, :] = part
     for h in range(heads):
         cols = slice(h * HD, (h + 1) * HD)
-        gwk_ref[:, cols] = tn(pulled_ref[h], q_ref[:, cols]).astype(BF16)
-
-
-def attention_calls(slots, queries, d_mixed, w_key, w_value, nbr_count):
+        of_value = tn(mixing_ref[h], dm_ref[:, cols])
+        of_key = tn(pulled_ref[h], q_ref[:, cols])
+        depth = of_key.shape[0] // shares
+        for d in range(shares):
+            part = slice(d * depth, (d + 1) * depth)
+            both = jnp.concatenate([of_value[part], of_key[part]], axis=0)
+            gwkv_ref[d, :, cols] = both.astype(BF16)
+
+
+def attention_setup(slots, queries):
     groups, key_len, enc = slots.shape
     tok_rows, width = queries.shape
     heads = min(4, width // HD)
     steps = width // (heads * HD)
     part = heads * HD
     group_rows = heads * (tok_rows // groups)
-    whole = pl.BlockSpec((groups, key_len, enc), lambda i: (0, 0, 0))
-    tok = pl.BlockSpec((tok_rows, part), lambda i: (0, i))
-    weight = pl.BlockSpec((enc, part), lambda i: (0, i))
-    prob = pl.BlockSpec((1, groups, group_rows, key_len), lambda i: (i, 0, 0, 0))
-    tok_shape = jax.ShapeDtypeStruct((tok_rows, width), BF16)
-    weight_shape = jax.ShapeDtypeStruct((enc, width), BF16)
-    prob_shape = jax.ShapeDtypeStruct((steps, groups, group_rows, key_len), BF16)
-    cost = pl.CostEstimate(
-        flops=int(4 * groups * group_rows * key_len * enc * steps * 1.2),
-        bytes_accessed=20_000_000,
-        transcendentals=groups * group_rows * steps * key_len,
+    specs = dict(
+        whole=pl.BlockSpec((groups, key_len, enc), lambda i: (0, 0, 0)),
+        tok=pl.BlockSpec((tok_rows, part), lambda i: (0, i)),
+        weight=pl.BlockSpec((enc, part), lambda i: (0, i)),
+        prob=pl.BlockSpec((1, groups, group_rows, key_len), lambda i: (i, 0, 0, 0)),
+        pull=pl.BlockSpec((heads, tok_rows, enc), lambda i: (i, 0, 0)),
+    )
+    shapes = dict(
+        tok=jax.ShapeDtypeStruct((tok_rows, width), BF16),
+        prob=jax.ShapeDtypeStruct((steps, groups, group_rows, key_len), BF16),
+        pull=jax.ShapeDtypeStruct((width // HD, tok_rows, enc), BF16),
     )
     common = dict(
         grid=(steps,),
+        compiler_params=pltpu.CompilerParams(vmem_limit_bytes=VMEM_LIMIT),
+        cost_estimate=pl.CostEstimate(
+            flops=int(4 * groups * group_rows * key_len * enc * steps * 1.2),
+            bytes_accessed=20_000_000,
+            transcendentals=groups * group_rows * steps * key_len,
+        ),
+    )
+    return groups, heads, specs, shapes, common
+
+
+def attend(slots, queries, w_key, w_value, nbr_count):
+    groups, heads, specs, shapes, common = attention_setup(slots, queries)
+    return pl.pallas_call(
+        functools.partial(forward_kernel, groups, heads),
+        in_specs=[pl.BlockSpec(memory_space=pltpu.SMEM)]
+        + [specs[n] for n in ("whole", "tok", "weight", "weight")],
+        out_specs=[specs[n] for n in ("tok", "prob", "pull")],
+        out_shape=[shapes[n] for n in ("tok", "prob", "pull")],
+        **common,
+    )(nbr_count, slots, queries, w_key, w_value)
+
+
+def attend_back(slots, queries, d_mixed, w_key, w_value, probs, mixing, shares):
+    groups, heads, specs, shapes, common = attention_setup(slots, queries)
+    tok_rows, width = queries.shape
+    enc = slots.shape[2]
+    rows = 2 * enc // shares
+    return pl.pallas_call(
+        functools.partial(backward_kernel, groups, heads, shares),
+        in_specs=[specs[n] for n in ("whole", "tok", "tok", "weight", "weight", "prob", "pull")],
+        out_specs=[
+            specs["tok"],
+            pl.BlockSpec((shares, rows, heads * HD), lambda i: (0, 0, i)),
+        ],
+        out_shape=[shapes["tok"], jax.ShapeDtypeStruct((shares, rows, width), BF16)],
         scratch_shapes=[pltpu.VMEM((heads, tok_rows, enc), BF16)],
-        compiler_params=pltpu.CompilerParams(vmem_limit_bytes=VMEM_LIMIT),
-        cost_estimate=cost,
-    )
-    mixed, probs, gwv = pl.pallas_call(
-        functools.partial(forward_kernel, groups, heads),
-        in_specs=[pl.BlockSpec(memory_space=pltpu.SMEM), whole, tok, tok, weight, weight],
-        out_specs=[tok, prob, weight],
-        out_shape=[tok_shape, prob_shape, weight_shape],
         **common,
-    )(nbr_count, slots, queries, d_mixed, w_key, w_value)
-    gq, gwk = pl.pallas_call(
-        functools.partial(backward_kernel, groups, heads),
-        in_specs=[whole, tok, tok, weight, weight, prob],
-        out_specs=[tok, weight],
-        out_shape=[tok_shape, weight_shape],
-        **common,
-    )(slots, queries, d_mixed, w_key, w_value, probs)
-    return mixed, gwv, gq, gwk
+    )(slots, queries, d_mixed, w_key, w_value, probs, mixing)
+
+
+class Track:
+    def __init__(self, me, source, tail, order, buffers, buffer_tail, finish):
+        self.me, self.cur, self.tail, self.order = me, source, tail, order
+        self.bits = sorted(order, reverse=True)
+        self.buffers, self.buffer_tail, self.finish = buffers, buffer_tail, finish
+        self.stage = 0
+        self.copy = None
+
+    def start(self, send_sem, recv_sem):
+        bit = self.order[self.stage]
+        mine = lax.rem(self.me // (1 << bit), 2)
+        lead = [slice(None)] * len(self.bits)
+        lead[self.bits.index(bit)] = 1 - mine
+        free = (slice(None),) * (len(self.bits) - 1)
+        self.copy = pltpu.make_async_remote_copy(
+            src_ref=self.cur.at[tuple(lead) + self.tail],
+            dst_ref=self.buffers[self.stage].at[free + self.buffer_tail],
+            send_sem=send_sem,
+            recv_sem=recv_sem,
+            device_id={"db": self.me + (1 - 2 * mine) * (1 << bit)},
+            device_id_type=pl.DeviceIdType.MESH,
+        )
+        self.copy.start()
+        return self.copy
+
+    def add(self):
+        self.copy.wait_recv()
+        bit = self.order[self.stage]
+        mine = lax.rem(self.me // (1 << bit), 2)
+        place = self.bits.index(bit)
+        buffer = self.buffers[self.stage]
+        last = self.stage == len(self.order) - 1
+        for rest in itertools.product(range(2), repeat=len(self.bits) - 1):
+            keep = rest[:place] + (mine,) + rest[place:]
+            total = self.cur[keep + self.tail].astype(F32) + buffer[
+                rest + self.buffer_tail
+            ].astype(F32)
+            if last:
+                self.finish(total)
+            else:
+                buffer[rest + self.buffer_tail] = total.astype(BF16)
+        self.bits.remove(bit)
+        self.cur, self.tail = buffer, self.buffer_tail
+        self.stage += 1
+        return last
+
+
+def reduce_kernel(all_bits, low_bits, kv_ref, wo_ref, gv_ref, gk_ref, gwo_ref, *scratch):
+    me = lax.axis_index("db")
+    kv_bufs = (scratch[0:all_bits], scratch[all_bits:2 * all_bits])
+    at = 2 * all_bits
+    wo_bufs = (scratch[at:at + low_bits], scratch[at + low_bits:at + 2 * low_bits])
+    send_sem, recv_sem = scratch[-2:]
+
+    barrier = pltpu.get_barrier_semaphore()
+    for bit in range(all_bits):
+        mine = lax.rem(me // (1 << bit), 2)
+        pl.semaphore_signal(
+            barrier,
+            inc=1,
+            device_id={"db": me + (1 - 2 * mine) * (1 << bit)},
+            device_id_type=pl.DeviceIdType.MESH,
+        )
+    pl.semaphore_wait(barrier, all_bits)
+
+    depth = gv_ref.shape[0]
+    half = kv_ref.shape[-1] // 2
+    chunks = min(4, half // 128)
+    size = half // chunks
+    rows_half = wo_ref.shape[-2] // 2
+    wo_size = rows_half // chunks
+    rounds = []
+    for c in range(chunks):
+        pair = []
+        for t in range(2):
+            order = list(range(all_bits))
+            if t == 1:
+                order[0], order[1] = order[1], order[0]
+            cols = slice(t * half + c * size, t * half + (c + 1) * size)
+
+            def finish(total, cols=cols):
+                gv_ref[:, cols] = total[:depth]
+                gk_ref[:, cols] = total[depth:]
+
+            pair.append(
+                Track(me, kv_ref, (slice(None), cols), order, kv_bufs[t],
+                      (slice(None), slice(c * size, (c + 1) * size)), finish)
+            )
+        rounds.append(pair)
+    for c in range(chunks):
+        pair = []
+        for t in range(2):
+            order = list(range(low_bits))
+            if t == 1:
+                order[0], order[1] = order[1], order[0]
+            rows = slice(t * rows_half + c * wo_size, t * rows_half + (c + 1) * wo_size)
+
+            def finish(total, rows=rows):
+                gwo_ref[rows, :] = total
+
+            pair.append(
+                Track(me, wo_ref, (rows, slice(None)), order, wo_bufs[t],
+                      (slice(c * wo_size, (c + 1) * wo_size), slice(None)), finish)
+            )
+        rounds.append(pair)
+
+    copies = []
+
+    def start(track):
+        k = len(copies)
+        copies.append(track.start(send_sem.at[k], recv_sem.at[k]))
+
+    for track in rounds[0]:
+        start(track)
+    active = []
+    for t in range(len(rounds) + all_bits):
+        if t < len(rounds):
+            active.append(rounds[t])
+        if t + 1 < len(rounds):
+            for track in rounds[t + 1]:
+                start(track)
+        for pair in list(active):
+            for track in pair:
+                if track.add():
+                    if pair in active:
+                        active.remove(pair)
+                else:
+                    start(track)
+    for copy in copies:
+        copy.wait_send()
+
+
+def reduce_scatter(gwkv, gwo):
+    shares, rows, width = gwkv.shape
+    low, out_rows, out_cols = gwo.shape
+    all_bits, low_bits = shares.bit_length() - 1, low.bit_length() - 1
+    kv_half, wo_half = width // 2, out_rows // 2
+    chunks = min(4, kv_half // 128)
+    kv_bufs = [
+        pltpu.VMEM((2,) * (all_bits - s - 1) + (rows, kv_half), BF16) for s in range(all_bits)
+    ]
+    wo_bufs = [
+        pltpu.VMEM((2,) * (low_bits - s - 1) + (wo_half, out_cols), BF16) for s in range(low_bits)
+    ]
+    n_copies = 2 * chunks * (all_bits + low_bits)
+    in_vmem = pl.BlockSpec(memory_space=pltpu.VMEM)
+    return pl.pallas_call(
+        functools.partial(reduce_kernel, all_bits, low_bits),
+        in_specs=[in_vmem, in_vmem],
+        out_specs=[in_vmem] * 3,
+        out_shape=[
+            jax.ShapeDtypeStruct((rows // 2, width), F32),
+            jax.ShapeDtypeStruct((rows // 2, width), F32),
+            jax.ShapeDtypeStruct((out_rows, out_cols), F32),
+        ],
+        scratch_shapes=kv_bufs + kv_bufs + wo_bufs + wo_bufs
+        + [pltpu.SemaphoreType.DMA((n_copies,)), pltpu.SemaphoreType.DMA((n_copies,))],
+        compiler_params=pltpu.CompilerParams(
+            collective_id=0, has_side_effects=True, vmem_limit_bytes=VMEM_LIMIT
+        ),
+        cost_estimate=pl.CostEstimate(
+            flops=gwkv.size, bytes_accessed=300_000_000, transcendentals=0
+        ),
+    )(
+        gwkv.reshape((2,) * all_bits + (rows, width)),
+        gwo.reshape((2,) * low_bits + (out_rows, out_cols)),
+    )
 
 
 def shards(queries, w_key, w_value, w_out, encodings, nbr_row, nbr_owner, nbr_count, grad_out):
@@ -150,20 +342,33 @@
     d_mixed = lax.dot_general(
         piece, w_out, (((1,), (1,)), ((), ())), preferred_element_type=F32
     ).astype(BF16)
-    out_cols = lax.all_to_all(piece, "db", split_axis=1, concat_axis=0, tiled=True)
+    low = 1 << ((db_count.bit_length() - 1) // 2)
+    lines = [list(range(first, db_count, low)) for first in range(low)]
+    out_cols = lax.all_to_all(
+        piece, "db", split_axis=1, concat_axis=0, axis_index_groups=lines, tiled=True
+    )
     picks = nbr_owner * groups + lax.broadcasted_iota(jnp.int32, nbr_owner.shape, 0)
     mine = jnp.take(received, picks.reshape(-1), axis=0, mode="clip")
     slots = lax.all_gather(mine, "head", axis=1, tiled=True)
     slots = slots.reshape(groups, slot_count * slice_len * head_count, enc_width)
-    mixed, gwv, gq, gwk = attention_calls(slots, queries, d_mixed, w_key, w_value, nbr_count)
-    mixed_all = lax.all_gather(mixed, "db", axis=0, tiled=True)
+    mixed, probs, mixing = attend(slots, queries, w_key, w_value, nbr_count)
+    line_mixed = lax.all_gather(mixed, "db", axis=0, axis_index_groups=lines, tiled=True)
     out_term = jnp.dot(mixed, w_out, preferred_element_type=F32)
     attended = lax.psum_scatter(out_term.astype(BF16), "head", scatter_dimension=1, tiled=True)
-    grad_wo = lax.dot_general(
-        mixed_all, out_cols, (((0,), (0,)), ((), ())), preferred_element_type=F32
-    )
-    grad_wv = lax.psum_scatter(gwv, "db", scatter_dimension=0, tiled=True).astype(F32)
-    grad_wk = lax.psum_scatter(gwk, "db", scatter_dimension=0, tiled=True).astype(F32)
+    gq, gwkv = attend_back(slots, queries, d_mixed, w_key, w_value, probs, mixing, db_count)
+    block = out_cols.shape[1] // low
+    line_wo = jnp.stack(
+        [
+            lax.dot_general(
+                line_mixed,
+                out_cols[:, d * block:(d + 1) * block],
+                (((0,), (0,)), ((), ())),
+                preferred_element_type=F32,
+            ).astype(BF16)
+            for d in range(low)
+        ]
+    )
+    grad_wv, grad_wk, grad_wo = reduce_scatter(gwkv, line_wo)
     return (attended, gq, grad_wk, grad_wv, grad_wo)
 
 

time: 471 us -> 361 us (0.77)
  waiting for transfers between devices: 342 us -> 130 us
  Pallas kernels: 41.9 us -> 143 us
  local copies, waits for them, and re-layouts: 11.9 us -> 18.6 us
    reduce_scatter x2 -> x0, waiting for transfers between devices: 124 us -> none  [the longest x1 84.9 us: shards(): lax.psum_scatter(gwk, 'db', scatter_dimension=0, tiled=True).astype(F32)]
    all_gather x1, waiting for transfers between devices: 113 us -> 0.01 us  [shards(): lax.all_gather(mixed, 'db', axis=0, axis_index_groups=lines, tiled=True)]
    pallas_call x2 -> x3, Pallas kernels: 41.9 us -> 143 us  [the longest x1 100 us: reduce_scatter(): pl.pallas_call(functools.partial(reduce_kernel, all_bits, low_bits), in_s...]
    all_to_all x1, waiting for transfers between devices: 22.8 us -> 38.3 us  [shards(): lax.all_to_all(piece, 'db', split_axis=1, concat_axis=0, axis_index_group...]
    all_gather x1, waiting for transfers between devices: 10.7 us -> 22.3 us  [shards(): slots = lax.all_gather(mine, 'head', axis=1, tiled=True)]
    unnamed x7 -> x12, local copies, waits for them, and re-layouts: 1.01 us -> 7.69 us
  transfers between devices with their start and end apart: 8 -> 6, of which waited for: 7 -> 3; matrix products, arithmetic and copies ran while one was open for 8% -> 9% of each run, Pallas kernels for 4% -> 40%
where the time goes in v2:
time: 361 us
  Pallas kernels  143 us (40%)
  waiting for transfers between devices  130 us (36%)
  matrix products  27.1 us (8%)
  local copies, waits for them, and re-layouts  18.6 us (5%)
  blocking collectives  15.4 us (4%)
  between operations  13.9 us (4%)
  starting transfers between devices  9.64 us (3%)
    pallas_call x1, Pallas kernels, reduce_scatter(): pl.pallas_call(functools.partial(reduce_kernel, all_bits, low_bits), in_s...  100 us
    all_to_all x1, waiting for transfers between devices, shards(): lax.all_to_all(table, 'db', split_axis=0, concat_axis=0, tiled=True)  69.4 us
    all_to_all x1, waiting for transfers between devices, shards(): lax.all_to_all(piece, 'db', split_axis=1, concat_axis=0, axis_index_group...  38.3 us
    pallas_call x1, Pallas kernels, attend_back(): pl.pallas_call(functools.partial(backward_kernel, groups, heads, shares),...  22.8 us
    all_gather x1, waiting for transfers between devices, shards(): slots = lax.all_gather(mine, 'head', axis=1, tiled=True)  22.3 us
    pallas_call x1, Pallas kernels, attend(): pl.pallas_call(functools.partial(forward_kernel, groups, heads), in_specs...  19.7 us
    all_to_all x1, blocking collectives, shards(): lax.all_to_all(wanted, 'db', split_axis=1, concat_axis=1, tiled=True)  15.4 us
    dot_general x1, matrix products, shards(): lax.dot_general(piece, w_out, (((1,), (1,)), ((), ())), preferred_element...  13.2 us
  transfers between devices with their start and end apart: 6, of which 3 were waited for; matrix products, arithmetic and copies ran while one was open for 9% of the time, Pallas kernels for 40%

profile of v2, /device:TPU:0, one launch (start us, length us, event | category | flops | bytes accessed | tf_op | source)
XLA Modules:
  0.0 360.7 jit_solution(12970977673951192746)
XLA Ops:
  7.2 0.8 select_reduce_fusion
  8.0 0.1 copy.24
  8.0 15.4 %all_to_all.36 = s32[2,16,1]{0,2,1:T(1,128)S(1)} all-to-all(s32[2,16,1]{0,2,1:T(1,128)S(1)} %copy.24), channel_id=1, replica_groups=mesh['db'=16,'head'=2] {'db'}, dimensions={1} | all-to-all | bytes 256 | tf_op jit(solution)/shard_map/all_to_all | solution.py:336
  23.4 0.1 copy.25
  23.5 0.1 copy.26
  23.6 0.1 reshape.43
  23.7 5.9 %gather_fusion = bf16[32,64,896]{2,1,0:T(8,128)(2,1)} fusion(bf16[64,64,896]{2,1,0:T(8,128)(2,1)} %param.13, s32[1024]{0:T(1024)S(1)} %pad_clamp_fusion.1), kind=kCustom, calls=%fused_computation | custom fusion | bytes 7340160 | tf_op jit(solution)/shard_map/jit(_take)/gather | solution.py:337
  29.6 0.0 copy-start.2
  29.6 4.6 %all-to-all-start.1 = ((bf16[16,128,896]{2,1,0:T(8,128)(2,1)}), bf16[16,128,896]{2,1,0:T(8,128)(2,1)}, u32[]{:S(2)}, u32[]{:S(2)}) async-start(bf16[16,128,896]{2,1,0:T(8,128)(2,1)} %bitcast.29), calls=%async_computation.1 | async-start | bytes 7340032 | tf_op jit(solution)/shard_map/all_to_all | solution.py:339
  34.2 0.0 copy-start.1
  34.2 0.0 all-gather.9.cloned.1.call-start
  34.3 0.0 copy-done.2
  34.3 0.1 reshape.51
  34.4 69.4 %all-to-all-done.1 = bf16[16,128,896]{2,1,0:T(8,128)(2,1)} async-done(((bf16[16,128,896]{2,1,0:T(8,128)(2,1)}), bf16[16,128,896]{2,1,0:T(8,128)(2,1)}, u32[]{:S(2)}, u32[]{:S(2)}) %all-to-all-start.1) | async-done | bytes 3670048 | tf_op jit(solution)/shard_map/all_to_all | solution.py:339
  103.8 4.0 %gather_fusion.1 = bf16[16,64,896]{2,1,0:T(8,128)(2,1)} fusion(bf16[32,64,896]{2,1,0:T(8,128)(2,1)} %bitcast.4, s32[1024]{0:T(1024)S(1)} %pad_clamp_fusion), kind=kCustom, calls=%fused_computation.1 | custom fusion | bytes 3670080 | tf_op jit(solution)/shard_map/jit(_take)/gather | solution.py:351
  107.8 0.0 all-gather.9.cloned.1.call-update
  107.8 0.0 all-gather.5.cloned.1.call-start
  107.9 0.0 copy-done.1
  107.9 1.0 copy.27
  108.9 0.0 all-gather.5.cloned.1.call-update
  108.9 0.0 all-gather.7.cloned.1.call-start
  109.0 22.3 %all-gather.9.cloned.1.call-done = bf16[16,128,896]{2,1,0:T(8,128)(2,1)} async-done(((bf16[16,64,896]{2,1,0:T(8,128)(2,1)}), bf16[16,128,896]{2,1,0:T(8,128)(2,1)}) %all-gather.9.cloned.1.call-update) | async-done | bytes 3670032 | tf_op jit(solution)/shard_map/all_gather | solution.py:352
  131.3 19.7 %shard_map.128 = (bf16[128,2048]{1,0:T(8,128)(2,1)}, bf16[4,2,256,1024]{3,2,1,0:T(8,128)(2,1)}, bf16[16,128,896]{2,1,0:T(8,128)(2,1)}) custom-call(s32[2]{0:T(128)} %count_ref.1, bf16[2,1024,896]{2,1,0:T(8,128)(2,1)} %bitcast.39, bf16[128,2048]{1,0:T(8,128)(2,1)} %q_ref.3, bf16[896,2048]{1,0:T(8,128)(2,1)} %wk_ref.3, bf16[896,2048]{1,0:T(8,128)(2,1)} %wv_ref.3), custom_call_target="tpu_custom_call" | custom-call | flops 9019430912 | bytes 20000000 | tf_op jit(solution)/shard_map/pallas_call | solution.py:129
  150.9 0.0 all-gather.7.cloned.1.call-update
  151.0 0.0 all-gather.5.cloned.1.call-done
  151.0 4.9 %all-to-all-start.2 = ((bf16[128,4,1024]{0,2,1:T(8,128)(2,1)}), bf16[128,4,1024]{0,2,1:T(8,128)(2,1)S(1)}, u32[]{:S(2)}, u32[]{:S(2)}) async-start(bf16[128,4,1024]{0,2,1:T(8,128)(2,1)} %bitcast.31), calls=%async_computation.3 | async-start | bytes 2097152 | tf_op jit(solution)/shard_map/all_to_all | solution.py:347
  155.9 0.0 copy-start
  155.9 0.0 reduce-scatter.2.cloned.1.call-start
  155.9 13.2 %convolution_convert_fusion.5.dm_ref = bf16[128,2048]{1,0:T(8,128)(2,1)} fusion(bf16[128,4096]{0,1:T(8,128)(2,1)} %all-gather.5.cloned.1.call-done, bf16[2048,4096]{1,0:T(8,128)(2,1)} %param.12), kind=kOutput, calls=%fused_computation.12 | convolution fusion | flops 2147745792 | bytes 18350080 | tf_op jit(solution)/shard_map/dot_general | solution.py:342
  169.1 38.3 %all-to-all-done.2 = bf16[128,4,1024]{0,2,1:T(8,128)(2,1)S(1)} async-done(((bf16[128,4,1024]{0,2,1:T(8,128)(2,1)}), bf16[128,4,1024]{0,2,1:T(8,128)(2,1)S(1)}, u32[]{:S(2)}, u32[]{:S(2)}) %all-to-all-start.2) | async-done | bytes 1048608 | tf_op jit(solution)/shard_map/all_to_all | solution.py:347
  207.4 0.5 copy.28
  207.9 0.0 copy-done
  207.9 9.1 %convolution_convert_fusion = bf16[128,4096]{1,0:T(8,128)(2,1)} fusion(bf16[128,2048]{1,0:T(8,128)(2,1)S(1)} %copy-done, bf16[2048,4096]{1,0:T(8,128)(2,1)} %param.12), kind=kOutput, calls=%fused_computation.2 | convolution fusion | flops 2148007936 | bytes 18350080 | tf_op jit(solution)/shard_map/dot_general | solution.py:356
  217.0 0.0 reduce-scatter.2.cloned.1.call-update
  217.1 22.8 %shard_map.129 = (bf16[128,2048]{1,0:T(8,128)(2,1)}, bf16[16,112,2048]{2,1,0:T(8,128)(2,1)}) custom-call(bf16[2,1024,896]{2,1,0:T(8,128)(2,1)} %bitcast.40, bf16[128,2048]{1,0:T(8,128)(2,1)} %q_ref.3, bf16[128,2048]{1,0:T(8,128)(2,1)} %convolution_convert_fusion.5.dm_ref, bf16[896,2048]{1,0:T(8,128)(2,1)} %wk_ref.3, bf16[896,2048]{1,0:T(8,128)(2,1)} %wv_ref.3, ...), custom_call_target="tpu_custom_call" | custom-call | flops 9019430912 | bytes 20000000 | tf_op jit(solution)/shard_map/pallas_call | solution.py:144
  239.9 0.0 all-gather.7.cloned.1.call-done
  239.9 0.0 copy-start.3
  239.9 2.5 fusion.3
  242.4 0.0 copy-done.3
  242.4 0.8 fusion.2
  243.2 0.8 fusion.1
  244.0 0.8 fusion
  244.7 2.3 pad_maximum_fusion
  247.1 100.4 %shard_map.130 = (f32[56,2048]{1,0:T(8,128)}, f32[56,2048]{1,0:T(8,128)}, f32[2048,256]{1,0:T(8,128)}) custom-call(bf16[2,2,2,2,112,2048]{5,4,3,2,1,0:T(8,128)(2,1)} %bitcast.30, bf16[2,2,2048,256]{3,2,1,0:T(8,128)(2,1)} %bitcast.28), custom_call_target="tpu_custom_call" | custom-call | flops 3670016 | bytes 300000000 | tf_op jit(solution)/shard_map/pallas_call | solution.py:303
  347.5 0.0 reduce-scatter.2.cloned.1.call-done
  347.5 1.8 copy.32
  349.3 1.8 copy.33
  351.1 3.0 copy.34
  (3 shorter events, 0.0 us)
Async XLA Ops:
  29.6 4.7 %copy-start.2 = (s32[2,8]{1,0:T(2,128)S(1)}, s32[2,8]{1,0:T(2,128)}, u32[]{:S(2)}) copy-start(s32[2,8]{1,0:T(2,128)} %param.15) | copy-start | bytes 196
  29.6 74.2 %all-to-all-start.1 = ((bf16[16,128,896]{2,1,0:T(8,128)(2,1)}), bf16[16,128,896]{2,1,0:T(8,128)(2,1)}, u32[]{:S(2)}, u32[]{:S(2)}) async-start(bf16[16,128,896]{2,1,0:T(8,128)(2,1)} %bitcast.29), calls=%async_computation.1 | async-start | bytes 7340032 | tf_op jit(solution)/shard_map/all_to_all | solution.py:339
  34.2 73.6 %copy-start.1 = (bf16[128,2048]{1,0:T(8,128)(2,1)S(1)}, bf16[128,2048]{1,0:T(8,128)(2,1)}, u32[]{:S(2)}) copy-start(bf16[128,2048]{1,0:T(8,128)(2,1)} %param.17) | copy-start | bytes 1572868
  34.2 97.0 %all-gather.9.cloned.1.call-start = ((), (), s32[]{:S(2)}) async-start(), calls=%async_computation.7 | async-start | bytes 5505024 | tf_op jit(solution)/shard_map/all_gather | solution.py:352
  107.8 43.2 %all-gather.5.cloned.1.call-start = ((), (), s32[]{:S(2)}) async-start(), calls=%async_computation.5 | async-start | bytes 1572864 | tf_op jit(solution)/shard_map/all_gather | solution.py:341
  108.9 131.0 %all-gather.7.cloned.1.call-start = ((), (), s32[]{:S(2)}) async-start(), calls=%async_computation.6 | async-start | bytes 2621440 | tf_op jit(solution)/shard_map/all_gather | solution.py:355
  151.0 56.4 %all-to-all-start.2 = ((bf16[128,4,1024]{0,2,1:T(8,128)(2,1)}), bf16[128,4,1024]{0,2,1:T(8,128)(2,1)S(1)}, u32[]{:S(2)}, u32[]{:S(2)}) async-start(bf16[128,4,1024]{0,2,1:T(8,128)(2,1)} %bitcast.31), calls=%async_computation.3 | async-start | bytes 2097152 | tf_op jit(solution)/shard_map/all_to_all | solution.py:347
  155.9 52.1 %copy-start = (bf16[128,2048]{1,0:T(8,128)(2,1)S(1)}, bf16[128,2048]{1,0:T(8,128)(2,1)}, u32[]{:S(2)}) copy-start(bf16[128,2048]{1,0:T(8,128)(2,1)} %get-tuple-element.13) | copy-start | bytes 1572868
  155.9 191.6 %reduce-scatter.2.cloned.1.call-start = ((), (), s32[]{:S(2)}) async-start(), calls=%async_computation.4 | async-start | bytes 1572864 | tf_op jit(solution)/shard_map/reduce_scatter | solution.py:357
  239.9 2.5 copy-start.3
Sparse Core Ops, SparseCore 0:
  107.9 23.2 all-gather.8
  133.4 10.1 all-gather.4
  151.1 65.1 all-gather.6
  218.9 7.6 reduce-scatter.1

commit v3 on v2

--- a/solution.py
+++ b/solution.py
@@ -201,11 +201,11 @@
         return last
 
 
-def reduce_kernel(all_bits, low_bits, kv_ref, wo_ref, gv_ref, gk_ref, gwo_ref, *scratch):
+def reduce_kernel(all_bits, wo_bits, kv_ref, wo_ref, gv_ref, gk_ref, gwo_ref, *scratch):
     me = lax.axis_index("db")
     kv_bufs = (scratch[0:all_bits], scratch[all_bits:2 * all_bits])
     at = 2 * all_bits
-    wo_bufs = (scratch[at:at + low_bits], scratch[at + low_bits:at + 2 * low_bits])
+    wo_bufs = (scratch[at:at + wo_bits], scratch[at + wo_bits:at + 2 * wo_bits])
     send_sem, recv_sem = scratch[-2:]
 
     barrier = pltpu.get_barrier_semaphore()
@@ -228,6 +228,7 @@
     rounds = []
     for c in range(chunks):
         pair = []
+        rounds.append(pair)
         for t in range(2):
             order = list(range(all_bits))
             if t == 1:
@@ -242,13 +243,10 @@
                 Track(me, kv_ref, (slice(None), cols), order, kv_bufs[t],
                       (slice(None), slice(c * size, (c + 1) * size)), finish)
             )
+        pair = []
         rounds.append(pair)
-    for c in range(chunks):
-        pair = []
         for t in range(2):
-            order = list(range(low_bits))
-            if t == 1:
-                order[0], order[1] = order[1], order[0]
+            order = list(range(all_bits - wo_bits, all_bits))
             rows = slice(t * rows_half + c * wo_size, t * rows_half + (c + 1) * wo_size)
 
             def finish(total, rows=rows):
@@ -258,7 +256,6 @@
                 Track(me, wo_ref, (rows, slice(None)), order, wo_bufs[t],
                       (slice(c * wo_size, (c + 1) * wo_size), slice(None)), finish)
             )
-        rounds.append(pair)
 
     copies = []
 
@@ -289,19 +286,19 @@
 def reduce_scatter(gwkv, gwo):
     shares, rows, width = gwkv.shape
     low, out_rows, out_cols = gwo.shape
-    all_bits, low_bits = shares.bit_length() - 1, low.bit_length() - 1
+    all_bits, wo_bits = shares.bit_length() - 1, low.bit_length() - 1
     kv_half, wo_half = width // 2, out_rows // 2
     chunks = min(4, kv_half // 128)
     kv_bufs = [
         pltpu.VMEM((2,) * (all_bits - s - 1) + (rows, kv_half), BF16) for s in range(all_bits)
     ]
     wo_bufs = [
-        pltpu.VMEM((2,) * (low_bits - s - 1) + (wo_half, out_cols), BF16) for s in range(low_bits)
+        pltpu.VMEM((2,) * (wo_bits - s - 1) + (wo_half, out_cols), BF16) for s in range(wo_bits)
     ]
-    n_copies = 2 * chunks * (all_bits + low_bits)
+    n_copies = 2 * chunks * (all_bits + wo_bits)
     in_vmem = pl.BlockSpec(memory_space=pltpu.VMEM)
     return pl.pallas_call(
-        functools.partial(reduce_kernel, all_bits, low_bits),
+        functools.partial(reduce_kernel, all_bits, wo_bits),
         in_specs=[in_vmem, in_vmem],
         out_specs=[in_vmem] * 3,
         out_shape=[
@@ -319,8 +316,133 @@
         ),
     )(
         gwkv.reshape((2,) * all_bits + (rows, width)),
-        gwo.reshape((2,) * low_bits + (out_rows, out_cols)),
-    )
+        gwo.reshape((2,) * wo_bits + (out_rows, out_cols)),
+    )
+
+
+def remote(source, target, send_sem, recv_sem, device):
+    copy = pltpu.make_async_remote_copy(
+        src_ref=source,
+        dst_ref=target,
+        send_sem=send_sem,
+        recv_sem=recv_sem,
+        device_id=device,
+        device_id_type=pl.DeviceIdType.MESH,
+    )
+    copy.start()
+    return copy
+
+
+def exchange_kernel(low, wanted_ref, grad_ref, incoming_ref, piece_ref, cols_ref,
+                    send_sem, recv_sem):
+    db_count, head_count = lax.axis_size("db"), lax.axis_size("head")
+    me, head = lax.axis_index("db"), lax.axis_index("head")
+    tokens, width = grad_ref.shape
+    high = db_count // low
+    block = width * head_count // db_count
+    lower, upper = lax.rem(me, low), me // low
+    barrier = pltpu.get_barrier_semaphore()
+    for k in range(1, db_count):
+        pl.semaphore_signal(barrier, inc=1, device_id={"db": lax.rem(me + k, db_count)},
+                            device_id_type=pl.DeviceIdType.MESH)
+    for k in range(1, head_count):
+        pl.semaphore_signal(barrier, inc=1, device_id={"head": lax.rem(head + k, head_count)},
+                            device_id_type=pl.DeviceIdType.MESH)
+    pl.semaphore_wait(barrier, db_count + head_count - 2)
+    copies = []
+    own = pl.ds(pl.multiple_of(head * width, width), width)
+    for k in range(1, head_count):
+        n = len(copies)
+        copies.append(remote(grad_ref, piece_ref.at[:, own], send_sem.at[n], recv_sem.at[n],
+                             {"head": lax.rem(head + k, head_count)}))
+    for k in range(1, db_count):
+        n = len(copies)
+        to = lax.rem(me + k, db_count)
+        copies.append(remote(wanted_ref.at[to], incoming_ref.at[me], send_sem.at[n],
+                             recv_sem.at[n], {"db": to}))
+    piece_ref[:, own] = grad_ref[...]
+    incoming_ref[me] = wanted_ref[me]
+    for copy in copies[:head_count - 1]:
+        copy.wait_recv()
+    rows = pl.ds(pl.multiple_of(lower * tokens, tokens), tokens)
+    for k in range(1, low):
+        to = lax.rem(lower + k, low)
+        for u in range(high):
+            n = len(copies)
+            cols = pl.ds(pl.multiple_of((u * low + to) * block, block), block)
+            copies.append(remote(piece_ref.at[:, cols],
+                                 cols_ref.at[rows, u * block:(u + 1) * block],
+                                 send_sem.at[n], recv_sem.at[n], {"db": upper * low + to}))
+    for u in range(high):
+        cols = pl.ds(pl.multiple_of((u * low + lower) * block, block), block)
+        cols_ref[rows, u * block:(u + 1) * block] = piece_ref[:, cols]
+    for copy in copies[head_count - 1:]:
+        copy.wait_recv()
+    for copy in copies:
+        copy.wait_send()
+
+
+def exchange(wanted, grad_out, low):
+    db_count, head_count = lax.axis_size("db"), lax.axis_size("head")
+    tokens, width = grad_out.shape
+    full = width * head_count
+    n = head_count - 1 + db_count - 1 + (low - 1) * (db_count // low)
+    in_vmem = pl.BlockSpec(memory_space=pltpu.VMEM)
+    return pl.pallas_call(
+        functools.partial(exchange_kernel, low),
+        in_specs=[in_vmem] * 2,
+        out_specs=[in_vmem] * 3,
+        out_shape=[
+            jax.ShapeDtypeStruct(wanted.shape, jnp.int32),
+            jax.ShapeDtypeStruct((tokens, full), BF16),
+            jax.ShapeDtypeStruct((low * tokens, full // low), BF16),
+        ],
+        scratch_shapes=[pltpu.SemaphoreType.DMA((n,)), pltpu.SemaphoreType.DMA((n,))],
+        compiler_params=pltpu.CompilerParams(
+            collective_id=1, has_side_effects=True, vmem_limit_bytes=VMEM_LIMIT
+        ),
+    )(wanted, grad_out)
+
+
+def share_kernel(mine_ref, whole_ref, send_sem, recv_sem, local_sem):
+    head_count, head = lax.axis_size("head"), lax.axis_index("head")
+    depth = mine_ref.shape[1]
+    barrier = pltpu.get_barrier_semaphore()
+    for k in range(1, head_count):
+        pl.semaphore_signal(barrier, inc=1, device_id={"head": lax.rem(head + k, head_count)},
+                            device_id_type=pl.DeviceIdType.MESH)
+    pl.semaphore_wait(barrier, head_count - 1)
+    place = whole_ref.at[:, pl.ds(pl.multiple_of(head * depth, depth), depth), :]
+    copies = [
+        remote(mine_ref, place, send_sem.at[k - 1], recv_sem.at[k - 1],
+               {"head": lax.rem(head + k, head_count)})
+        for k in range(1, head_count)
+    ]
+    local = pltpu.make_async_copy(mine_ref, place, local_sem)
+    local.start()
+    for copy in copies:
+        copy.wait()
+    local.wait()
+
+
+def share(mine):
+    head_count = lax.axis_size("head")
+    rows, depth, enc = mine.shape
+    in_vmem = pl.BlockSpec(memory_space=pltpu.VMEM)
+    return pl.pallas_call(
+        share_kernel,
+        in_specs=[in_vmem],
+        out_specs=in_vmem,
+        out_shape=jax.ShapeDtypeStruct((rows, depth * head_count, enc), BF16),
+        scratch_shapes=[
+            pltpu.SemaphoreType.DMA((head_count - 1,)),
+            pltpu.SemaphoreType.DMA((head_count - 1,)),
+            pltpu.SemaphoreType.DMA,
+        ],
+        compiler_params=pltpu.CompilerParams(
+            collective_id=2, has_side_effects=True, vmem_limit_bytes=VMEM_LIMIT
+        ),
+    )(mine)
 
 
 def shards(queries, w_key, w_value, w_out, encodings, nbr_row, nbr_owner, nbr_count, grad_out):
@@ -333,42 +455,42 @@
     owner_ids = lax.broadcasted_iota(jnp.int32, (1, 1, db_count), 2)
     chosen = nbr_owner[:, :, None] == owner_ids
     wanted = jnp.sum(jnp.where(chosen, nbr_row[:, :, None], 0), axis=1)
-    incoming = lax.all_to_all(wanted, "db", split_axis=1, concat_axis=1, tiled=True)
-    table = jnp.take(encodings, incoming.T.reshape(-1), axis=0, mode="clip")
+    low = 1 << ((db_count.bit_length() - 1) // 2)
+    planes = [list(range(first, first + low)) for first in range(0, db_count, low)]
+    padded = jnp.broadcast_to(
+        jnp.pad(wanted.T, ((0, 0), (0, 128 - groups)))[:, None, :], (db_count, 8, 128)
+    )
+    incoming, piece, out_cols = exchange(padded, grad_out, low)
+    table = jnp.take(encodings, incoming[:, 0, :groups].reshape(-1), axis=0, mode="clip")
     table = table.reshape(db_count, groups * slice_len, enc_width)
     received = lax.all_to_all(table, "db", split_axis=0, concat_axis=0, tiled=True)
-    received = received.reshape(db_count * groups, slice_len, enc_width)
-    piece = lax.all_gather(grad_out, "head", axis=1, tiled=True)
     d_mixed = lax.dot_general(
         piece, w_out, (((1,), (1,)), ((), ())), preferred_element_type=F32
     ).astype(BF16)
-    low = 1 << ((db_count.bit_length() - 1) // 2)
-    lines = [list(range(first, db_count, low)) for first in range(low)]
-    out_cols = lax.all_to_all(
-        piece, "db", split_axis=1, concat_axis=0, axis_index_groups=lines, tiled=True
-    )
+    received, d_mixed = lax.optimization_barrier((received, d_mixed))
+    received = received.reshape(db_count * groups, slice_len, enc_width)
     picks = nbr_owner * groups + lax.broadcasted_iota(jnp.int32, nbr_owner.shape, 0)
     mine = jnp.take(received, picks.reshape(-1), axis=0, mode="clip")
-    slots = lax.all_gather(mine, "head", axis=1, tiled=True)
-    slots = slots.reshape(groups, slot_count * slice_len * head_count, enc_width)
+    slots = share(mine).reshape(groups, slot_count * slice_len * head_count, enc_width)
     mixed, probs, mixing = attend(slots, queries, w_key, w_value, nbr_count)
-    line_mixed = lax.all_gather(mixed, "db", axis=0, axis_index_groups=lines, tiled=True)
+    plane_mixed = lax.all_gather(mixed, "db", axis=0, axis_index_groups=planes, tiled=True)
     out_term = jnp.dot(mixed, w_out, preferred_element_type=F32)
     attended = lax.psum_scatter(out_term.astype(BF16), "head", scatter_dimension=1, tiled=True)
     gq, gwkv = attend_back(slots, queries, d_mixed, w_key, w_value, probs, mixing, db_count)
-    block = out_cols.shape[1] // low
-    line_wo = jnp.stack(
+    high = db_count // low
+    block = out_cols.shape[1] // high
+    plane_wo = jnp.stack(
         [
             lax.dot_general(
-                line_mixed,
+                plane_mixed,
                 out_cols[:, d * block:(d + 1) * block],
                 (((0,), (0,)), ((), ())),
                 preferred_element_type=F32,
             ).astype(BF16)
-            for d in range(low)
+            for d in range(high)
         ]
     )
-    grad_wv, grad_wk, grad_wo = reduce_scatter(gwkv, line_wo)
+    grad_wv, grad_wk, grad_wo = reduce_scatter(gwkv, plane_wo)
     return (attended, gq, grad_wk, grad_wv, grad_wo)
 
 

time: 361 us -> 334 us (0.925)
  waiting for transfers between devices: 130 us -> 74.5 us
  Pallas kernels: 143 us -> 191 us
  blocking collectives: 15.4 us -> 0 us
  starting transfers between devices: 9.64 us -> 4.73 us
    pallas_call x1 -> x3, Pallas kernels: 100 us -> 148 us  [the longest x1 117 us: reduce_scatter(): pl.pallas_call(functools.partial(reduce_kernel, all_bits, wo_bits), in_sp...]
    all_to_all x1 -> x0, waiting for transfers between devices: 38.3 us -> none  [shards(): lax.all_to_all(piece, 'db', split_axis=1, concat_axis=0, axis_index_group...]
    all_to_all x1 -> x0, blocking collectives: 15.4 us -> none  [shards(): lax.all_to_all(wanted, 'db', split_axis=1, concat_axis=1, tiled=True)]
    all_to_all x1, waiting for transfers between devices: 69.4 us -> 58.6 us  [shards(): lax.all_to_all(table, 'db', split_axis=0, concat_axis=0, tiled=True)]
    all_gather x3 -> x1, waiting for transfers between devices: 22.3 us -> 15.8 us  [shards(): lax.all_gather(mixed, 'db', axis=0, axis_index_groups=planes, tiled=True)]
    all_to_all x1 -> x0, starting transfers between devices: 4.87 us -> none  [shards(): lax.all_to_all(piece, 'db', split_axis=1, concat_axis=0, axis_index_group...]
  transfers between devices with their start and end apart: 6 -> 3, of which waited for: 3 -> 2; matrix products, arithmetic and copies ran while one was open for 9% -> 9% of each run, Pallas kernels for 40% -> 42%
where the time goes in v3:
time: 334 us; the launch traced here: 333 us
  Pallas kernels  191 us (57%)
  waiting for transfers between devices  74.5 us (22%)
  matrix products  26.3 us (8%)
  local copies, waits for them, and re-layouts  18.3 us (5%)
  between operations  15.6 us (5%)
  starting transfers between devices  4.73 us (1%)
    pallas_call x1, Pallas kernels, reduce_scatter(): pl.pallas_call(functools.partial(reduce_kernel, all_bits, wo_bits), in_sp...  117 us
    all_to_all x1, waiting for transfers between devices, shards(): lax.all_to_all(table, 'db', split_axis=0, concat_axis=0, tiled=True)  58.6 us
    pallas_call x1, Pallas kernels, exchange(): pl.pallas_call(functools.partial(exchange_kernel, low), in_specs=[in_vmem...  24.2 us
    pallas_call x1, Pallas kernels, attend_back(): pl.pallas_call(functools.partial(backward_kernel, groups, heads, shares),...  23.1 us
    pallas_call x1, Pallas kernels, attend(): pl.pallas_call(functools.partial(forward_kernel, groups, heads), in_specs...  19.7 us
    all_gather x1, waiting for transfers between devices, shards(): lax.all_gather(mixed, 'db', axis=0, axis_index_groups=planes, tiled=True)  15.8 us
    dot_general x1, matrix products, shards(): lax.dot_general(piece, w_out, (((1,), (1,)), ((), ())), preferred_element...  12.2 us
    dot_general x1, matrix products, shards(): out_term = jnp.dot(mixed, w_out, preferred_element_type=F32)  9.27 us
  transfers between devices with their start and end apart: 3, of which 2 were waited for; matrix products, arithmetic and copies ran while one was open for 9% of the time, Pallas kernels for 42%

profile of v3, /device:TPU:0, one launch (start us, length us, event | category | flops | bytes accessed | tf_op | source)
XLA Modules:
  0.0 333.3 jit_solution(8256597747353051036)
XLA Ops:
  8.0 0.8 select_reduce_fusion
  8.8 0.1 copy.15
  8.9 0.6 broadcast_in_dim.30.wanted_ref
  9.5 24.2 %shard_map.128 = (s32[16,8,128]{2,1,0:T(8,128)}, bf16[128,4096]{1,0:T(8,128)(2,1)}, bf16[512,1024]{1,0:T(8,128)(2,1)}) custom-call(s32[16,8,128]{2,1,0:T(8,128)} %broadcast_in_dim.30.wanted_ref, bf16[128,2048]{1,0:T(8,128)(2,1)} %grad_ref.1), custom_call_target="tpu_custom_call" | custom-call | tf_op jit(solution)/shard_map/pallas_call | solution.py:391
  33.7 0.9 slice_reduce_fusion
  34.6 0.1 reshape.38
  34.7 5.9 %gather_fusion = bf16[32,64,896]{2,1,0:T(8,128)(2,1)} fusion(bf16[64,64,896]{2,1,0:T(8,128)(2,1)} %param.13, s32[1024]{0:T(1024)S(1)} %pad_clamp_fusion.1), kind=kCustom, calls=%fused_computation | custom fusion | bytes 7340160 | tf_op jit(solution)/shard_map/jit(_take)/gather | solution.py:464
  40.6 0.0 copy-start.1
  40.6 0.0 copy-start
  40.6 4.6 %all-to-all-start = ((bf16[16,128,896]{2,1,0:T(8,128)(2,1)}), bf16[16,128,896]{2,1,0:T(8,128)(2,1)}, u32[]{:S(2)}, u32[]{:S(2)}) async-start(bf16[16,128,896]{2,1,0:T(8,128)(2,1)} %bitcast.23), calls=%async_computation | async-start | bytes 7340032 | tf_op jit(solution)/shard_map/all_to_all | solution.py:466
  45.2 0.0 all-gather.2.cloned.1.call-start
  45.3 0.0 copy-done.1
  45.3 0.1 reshape.46
  45.4 0.0 copy-done
  45.4 12.2 %convolution_convert_fusion.5.dm_ref = bf16[128,2048]{1,0:T(8,128)(2,1)} fusion(bf16[128,4096]{1,0:T(8,128)(2,1)S(1)} %copy-done, bf16[2048,4096]{1,0:T(8,128)(2,1)} %param.12), kind=kOutput, calls=%fused_computation.12 | convolution fusion | flops 2147745792 | bytes 18350080 | tf_op jit(solution)/shard_map/dot_general | solution.py:467
  57.6 58.6 %all-to-all-done = bf16[16,128,896]{2,1,0:T(8,128)(2,1)} async-done(((bf16[16,128,896]{2,1,0:T(8,128)(2,1)}), bf16[16,128,896]{2,1,0:T(8,128)(2,1)}, u32[]{:S(2)}, u32[]{:S(2)}) %all-to-all-start) | async-done | bytes 3670048 | tf_op jit(solution)/shard_map/all_to_all | solution.py:466
  116.2 4.0 %gather_fusion.1 = bf16[16,64,896]{2,1,0:T(8,128)(2,1)} fusion(bf16[32,64,896]{2,1,0:T(8,128)(2,1)} %bitcast.2, s32[1024]{0:T(1024)S(1)} %pad_clamp_fusion), kind=kCustom, calls=%fused_computation.1 | custom fusion | bytes 3670080 | tf_op jit(solution)/shard_map/jit(_take)/gather | solution.py:473
  120.2 7.2 %shard_map.129 = bf16[16,128,896]{2,1,0:T(8,128)(2,1)} custom-call(bf16[16,64,896]{2,1,0:T(8,128)(2,1)} %gather_fusion.1), custom_call_target="tpu_custom_call" | custom-call | tf_op jit(solution)/shard_map/pallas_call | solution.py:432
  127.4 19.7 %shard_map.130 = (bf16[128,2048]{1,0:T(8,128)(2,1)}, bf16[4,2,256,1024]{3,2,1,0:T(8,128)(2,1)}, bf16[16,128,896]{2,1,0:T(8,128)(2,1)}) custom-call(s32[2]{0:T(128)} %count_ref.1, bf16[2,1024,896]{2,1,0:T(8,128)(2,1)} %bitcast.25, bf16[128,2048]{1,0:T(8,128)(2,1)} %q_ref.3, bf16[896,2048]{1,0:T(8,128)(2,1)} %wk_ref.3, bf16[896,2048]{1,0:T(8,128)(2,1)} %wv_ref.3), custom_call_target="tpu_custom_call" | custom-call | flops 9019430912 | bytes 20000000 | tf_op jit(solution)/shard_map/pallas_call | solution.py:129
  147.1 0.0 all-gather.2.cloned.1.call-update
  147.1 0.0 reduce-scatter.2.cloned.1.call-start
  147.2 9.3 %convolution_convert_fusion = bf16[128,4096]{1,0:T(8,128)(2,1)} fusion(bf16[128,2048]{1,0:T(8,128)(2,1)} %get-tuple-element.21, bf16[2048,4096]{1,0:T(8,128)(2,1)} %param.12), kind=kOutput, calls=%fused_computation.2 | convolution fusion | flops 2148007936 | bytes 18350080 | tf_op jit(solution)/shard_map/dot_general | solution.py:477
  156.5 0.0 reduce-scatter.2.cloned.1.call-update
  156.5 0.0 copy-start.3
  156.5 23.1 %shard_map.131 = (bf16[128,2048]{1,0:T(8,128)(2,1)}, bf16[16,112,2048]{2,1,0:T(8,128)(2,1)}) custom-call(bf16[2,1024,896]{2,1,0:T(8,128)(2,1)} %bitcast.26, bf16[128,2048]{1,0:T(8,128)(2,1)} %q_ref.3, bf16[128,2048]{1,0:T(8,128)(2,1)} %convolution_convert_fusion.5.dm_ref, bf16[896,2048]{1,0:T(8,128)(2,1)} %wk_ref.3, bf16[896,2048]{1,0:T(8,128)(2,1)} %wv_ref.3, ...), custom_call_target="tpu_custom_call" | custom-call | flops 9019430912 | bytes 20000000 | tf_op jit(solution)/shard_map/pallas_call | solution.py:144
  179.6 15.8 %all-gather.2.cloned.1.call-done = bf16[512,2048]{1,0:T(8,128)(2,1)} async-done(((bf16[128,2048]{1,0:T(8,128)(2,1)}), bf16[512,2048]{1,0:T(8,128)(2,1)}) %all-gather.2.cloned.1.call-update) | async-done | bytes 2097168 | tf_op jit(solution)/shard_map/all_gather | solution.py:476
  195.4 0.0 copy-start.2
  195.4 0.0 copy-done.3
  195.5 2.5 fusion.3
  198.0 0.0 copy-done.2
  198.0 0.8 fusion.2
  198.7 0.8 fusion.1
  199.5 0.8 fusion
  200.3 2.3 pad_maximum_fusion
  202.6 116.5 %shard_map.132 = (f32[56,2048]{1,0:T(8,128)}, f32[56,2048]{1,0:T(8,128)}, f32[2048,256]{1,0:T(8,128)}) custom-call(bf16[2,2,2,2,112,2048]{5,4,3,2,1,0:T(8,128)(2,1)} %bitcast.24, bf16[2,2,2048,256]{3,2,1,0:T(8,128)(2,1)} %bitcast.22), custom_call_target="tpu_custom_call" | custom-call | flops 3670016 | bytes 300000000 | tf_op jit(solution)/shard_map/pallas_call | solution.py:300
  319.1 0.0 reduce-scatter.2.cloned.1.call-done
  319.2 1.8 copy.19
  321.0 1.8 copy.20
  322.8 3.0 copy.21
  (4 shorter events, 0.0 us)
Async XLA Ops:
  40.6 4.7 %copy-start.1 = (s32[2,8]{1,0:T(2,128)S(1)}, s32[2,8]{1,0:T(2,128)}, u32[]{:S(2)}) copy-start(s32[2,8]{1,0:T(2,128)} %param.15) | copy-start | bytes 196
  40.6 4.8 %copy-start = (bf16[128,4096]{1,0:T(8,128)(2,1)S(1)}, bf16[128,4096]{1,0:T(8,128)(2,1)}, u32[]{:S(2)}) copy-start(bf16[128,4096]{1,0:T(8,128)(2,1)} %get-tuple-element.19) | copy-start | bytes 3145732
  40.6 75.6 %all-to-all-start = ((bf16[16,128,896]{2,1,0:T(8,128)(2,1)}), bf16[16,128,896]{2,1,0:T(8,128)(2,1)}, u32[]{:S(2)}, u32[]{:S(2)}) async-start(bf16[16,128,896]{2,1,0:T(8,128)(2,1)} %bitcast.23), calls=%async_computation | async-start | bytes 7340032 | tf_op jit(solution)/shard_map/all_to_all | solution.py:466
  45.2 150.2 %all-gather.2.cloned.1.call-start = ((), (), s32[]{:S(2)}) async-start(), calls=%async_computation.3 | async-start | bytes 2621440 | tf_op jit(solution)/shard_map/all_gather | solution.py:476
  147.1 172.0 %reduce-scatter.2.cloned.1.call-start = ((), (), s32[]{:S(2)}) async-start(), calls=%async_computation.2 | async-start | bytes 1572864 | tf_op jit(solution)/shard_map/reduce_scatter | solution.py:478
  156.5 39.0 %copy-start.3 = (bf16[512,1024]{1,0:T(8,128)(2,1)S(1)}, bf16[512,1024]{1,0:T(8,128)(2,1)}, u32[]{:S(2)}) copy-start(bf16[512,1024]{1,0:T(8,128)(2,1)} %get-tuple-element.27) | copy-start | bytes 3145732
  195.4 2.5 copy-start.2
Sparse Core Ops, SparseCore 0:
  147.3 48.1 all-gather.1
Sparse Core Ops, SparseCore 1:
  156.6 21.3 reduce-scatter.1

commit v4 on v3

--- a/solution.py
+++ b/solution.py
@@ -263,22 +263,21 @@
         k = len(copies)
         copies.append(track.start(send_sem.at[k], recv_sem.at[k]))
 
-    for track in rounds[0]:
-        start(track)
+    for pair in rounds[0:2] + rounds[3::2] + rounds[2:3]:
+        for track in pair:
+            start(track)
     active = []
     for t in range(len(rounds) + all_bits):
-        if t < len(rounds):
-            active.append(rounds[t])
-        if t + 1 < len(rounds):
-            for track in rounds[t + 1]:
+        active += rounds[t:t + 1]
+        if t % 2 == 0 and t + 4 < len(rounds):
+            for track in rounds[t + 4]:
                 start(track)
         for pair in list(active):
             for track in pair:
-                if track.add():
-                    if pair in active:
-                        active.remove(pair)
-                else:
+                if not track.add():
                     start(track)
+                elif pair in active:
+                    active.remove(pair)
     for copy in copies:
         copy.wait_send()
 
@@ -333,40 +332,48 @@
     return copy
 
 
-def exchange_kernel(low, wanted_ref, grad_ref, incoming_ref, piece_ref, cols_ref,
-                    send_sem, recv_sem):
+def greet(db_peers, head_peers):
+    barrier = pltpu.get_barrier_semaphore()
+    for device in [{"db": d} for d in db_peers] + [{"head": h} for h in head_peers]:
+        pl.semaphore_signal(barrier, inc=1, device_id=device,
+                            device_id_type=pl.DeviceIdType.MESH)
+    pl.semaphore_wait(barrier, len(db_peers) + len(head_peers))
+
+
+def request_kernel(wanted_ref, incoming_ref, send_sem, recv_sem):
+    db_count, me = lax.axis_size("db"), lax.axis_index("db")
+    peers = [lax.rem(me + k, db_count) for k in range(1, db_count)]
+    greet(peers, [])
+    copies = [
+        remote(wanted_ref.at[to], incoming_ref.at[me], send_sem.at[n], recv_sem.at[n], {"db": to})
+        for n, to in enumerate(peers)
+    ]
+    incoming_ref[me] = wanted_ref[me]
+    for copy in copies:
+        copy.wait()
+
+
+def exchange_kernel(low, grad_ref, piece_ref, cols_ref, send_sem, recv_sem):
     db_count, head_count = lax.axis_size("db"), lax.axis_size("head")
     me, head = lax.axis_index("db"), lax.axis_index("head")
     tokens, width = grad_ref.shape
     high = db_count // low
     block = width * head_count // db_count
     lower, upper = lax.rem(me, low), me // low
-    barrier = pltpu.get_barrier_semaphore()
-    for k in range(1, db_count):
-        pl.semaphore_signal(barrier, inc=1, device_id={"db": lax.rem(me + k, db_count)},
-                            device_id_type=pl.DeviceIdType.MESH)
-    for k in range(1, head_count):
-        pl.semaphore_signal(barrier, inc=1, device_id={"head": lax.rem(head + k, head_count)},
-                            device_id_type=pl.DeviceIdType.MESH)
-    pl.semaphore_wait(barrier, db_count + head_count - 2)
+    near = [lax.rem(lower + k, low) for k in range(1, low)]
+    heads = [lax.rem(head + k, head_count) for k in range(1, head_count)]
+    greet([upper * low + to for to in near], heads)
     copies = []
     own = pl.ds(pl.multiple_of(head * width, width), width)
-    for k in range(1, head_count):
+    for to in heads:
         n = len(copies)
         copies.append(remote(grad_ref, piece_ref.at[:, own], send_sem.at[n], recv_sem.at[n],
-                             {"head": lax.rem(head + k, head_count)}))
-    for k in range(1, db_count):
-        n = len(copies)
-        to = lax.rem(me + k, db_count)
-        copies.append(remote(wanted_ref.at[to], incoming_ref.at[me], send_sem.at[n],
-                             recv_sem.at[n], {"db": to}))
+                             {"head": to}))
     piece_ref[:, own] = grad_ref[...]
-    incoming_ref[me] = wanted_ref[me]
-    for copy in copies[:head_count - 1]:
+    for copy in copies:
         copy.wait_recv()
     rows = pl.ds(pl.multiple_of(lower * tokens, tokens), tokens)
-    for k in range(1, low):
-        to = lax.rem(lower + k, low)
+    for to in near:
         for u in range(high):
             n = len(copies)
             cols = pl.ds(pl.multiple_of((u * low + to) * block, block), block)
@@ -382,18 +389,30 @@
         copy.wait_send()
 
 
-def exchange(wanted, grad_out, low):
+def request(wanted):
+    n = lax.axis_size("db") - 1
+    in_vmem = pl.BlockSpec(memory_space=pltpu.VMEM)
+    return pl.pallas_call(
+        request_kernel,
+        in_specs=[in_vmem],
+        out_specs=in_vmem,
+        out_shape=jax.ShapeDtypeStruct(wanted.shape, jnp.int32),
+        scratch_shapes=[pltpu.SemaphoreType.DMA((n,)), pltpu.SemaphoreType.DMA((n,))],
+        compiler_params=pltpu.CompilerParams(collective_id=3, has_side_effects=True),
+    )(wanted)
+
+
+def exchange(grad_out, low):
     db_count, head_count = lax.axis_size("db"), lax.axis_size("head")
     tokens, width = grad_out.shape
     full = width * head_count
-    n = head_count - 1 + db_count - 1 + (low - 1) * (db_count // low)
+    n = head_count - 1 + (low - 1) * (db_count // low)
     in_vmem = pl.BlockSpec(memory_space=pltpu.VMEM)
     return pl.pallas_call(
         functools.partial(exchange_kernel, low),
-        in_specs=[in_vmem] * 2,
-        out_specs=[in_vmem] * 3,
+        in_specs=[in_vmem],
+        out_specs=[in_vmem] * 2,
         out_shape=[
-            jax.ShapeDtypeStruct(wanted.shape, jnp.int32),
             jax.ShapeDtypeStruct((tokens, full), BF16),
             jax.ShapeDtypeStruct((low * tokens, full // low), BF16),
         ],
@@ -401,7 +420,8 @@
         compiler_params=pltpu.CompilerParams(
             collective_id=1, has_side_effects=True, vmem_limit_bytes=VMEM_LIMIT
         ),
-    )(wanted, grad_out)
+        cost_estimate=pl.CostEstimate(flops=0, bytes_accessed=40_000_000, transcendentals=0),
+    )(grad_out)
 
 
 def share_kernel(mine_ref, whole_ref, send_sem, recv_sem, local_sem):
@@ -460,14 +480,15 @@
     padded = jnp.broadcast_to(
         jnp.pad(wanted.T, ((0, 0), (0, 128 - groups)))[:, None, :], (db_count, 8, 128)
     )
-    incoming, piece, out_cols = exchange(padded, grad_out, low)
+    incoming = request(padded)
     table = jnp.take(encodings, incoming[:, 0, :groups].reshape(-1), axis=0, mode="clip")
     table = table.reshape(db_count, groups * slice_len, enc_width)
     received = lax.all_to_all(table, "db", split_axis=0, concat_axis=0, tiled=True)
+    piece, out_cols = exchange(lax.optimization_barrier((grad_out, table))[0], low)
     d_mixed = lax.dot_general(
         piece, w_out, (((1,), (1,)), ((), ())), preferred_element_type=F32
     ).astype(BF16)
-    received, d_mixed = lax.optimization_barrier((received, d_mixed))
+    received, d_mixed, out_cols = lax.optimization_barrier((received, d_mixed, out_cols))
     received = received.reshape(db_count * groups, slice_len, enc_width)
     picks = nbr_owner * groups + lax.broadcasted_iota(jnp.int32, nbr_owner.shape, 0)
     mine = jnp.take(received, picks.reshape(-1), axis=0, mode="clip")

time: 334 us -> 329 us (0.985)
  waiting for transfers between devices: 74.5 us -> 28.2 us
  Pallas kernels: 191 us -> 228 us
    all_to_all x1, waiting for transfers between devices: 58.6 us -> 15 us  [shards(): lax.all_to_all(table, 'db', split_axis=0, concat_axis=0, tiled=True)]
    pallas_call x1, Pallas kernels: 24.2 us -> 42.3 us  [exchange(): pl.pallas_call(functools.partial(exchange_kernel, low), in_specs=[in_vmem...]
    pallas_call x0 -> x1, Pallas kernels: none -> 11.2 us  [request(): pl.pallas_call(request_kernel, in_specs=[in_vmem], out_specs=in_vmem, out...]
    pallas_call x1, Pallas kernels: 117 us -> 124 us  [reduce_scatter(): pl.pallas_call(functools.partial(reduce_kernel, all_bits, wo_bits), in_sp...]
    unnamed x12 -> x10, local copies, waits for them, and re-layouts: 6.78 us -> 6.77 us
  transfers between devices with their start and end apart: 3 -> 3, of which waited for: 2 -> 2; matrix products, arithmetic and copies ran while one was open for 9% -> 9% of each run, Pallas kernels for 42% -> 58%
where the time goes in v4:
time: 329 us; the launch traced here: 327 us
  Pallas kernels  228 us (69%)
  waiting for transfers between devices  28.2 us (9%)
  matrix products  26.6 us (8%)
  local copies, waits for them, and re-layouts  18.3 us (6%)
  between operations  15.6 us (5%)
  starting transfers between devices  6.8 us (2%)
    pallas_call x1, Pallas kernels, reduce_scatter(): pl.pallas_call(functools.partial(reduce_kernel, all_bits, wo_bits), in_sp...  124 us
    pallas_call x1, Pallas kernels, exchange(): pl.pallas_call(functools.partial(exchange_kernel, low), in_specs=[in_vmem...  42.3 us
    pallas_call x1, Pallas kernels, attend_back(): pl.pallas_call(functools.partial(backward_kernel, groups, heads, shares),...  23.1 us
    pallas_call x1, Pallas kernels, attend(): pl.pallas_call(functools.partial(forward_kernel, groups, heads), in_specs...  19.7 us
    all_to_all x1, waiting for transfers between devices, shards(): lax.all_to_all(table, 'db', split_axis=0, concat_axis=0, tiled=True)  15 us
    all_gather x1, waiting for transfers between devices, shards(): lax.all_gather(mixed, 'db', axis=0, axis_index_groups=planes, tiled=True)  13.1 us
    dot_general x1, matrix products, shards(): lax.dot_general(piece, w_out, (((1,), (1,)), ((), ())), preferred_element...  12.6 us
    pallas_call x1, Pallas kernels, request(): pl.pallas_call(request_kernel, in_specs=[in_vmem], out_specs=in_vmem, out...  11.2 us
  transfers between devices with their start and end apart: 3, of which 2 were waited for; matrix products, arithmetic and copies ran while one was open for 9% of the time, Pallas kernels for 58%

profile of v4, /device:TPU:0, one launch (start us, length us, event | category | flops | bytes accessed | tf_op | source)
XLA Modules:
  0.0 326.7 jit_solution(18104567737942071129)
XLA Ops:
  8.0 0.8 select_reduce_fusion
  8.8 0.1 copy.15
  8.9 0.6 broadcast_in_dim.30.wanted_ref
  9.5 11.2 %shard_map.128 = s32[16,8,128]{2,1,0:T(8,128)} custom-call(s32[16,8,128]{2,1,0:T(8,128)} %broadcast_in_dim.30.wanted_ref), custom_call_target="tpu_custom_call" | custom-call | tf_op jit(solution)/shard_map/pallas_call | solution.py:395
  20.7 0.9 slice_reduce_fusion
  21.6 0.1 reshape.38
  21.7 5.9 %gather_fusion = bf16[32,64,896]{2,1,0:T(8,128)(2,1)} fusion(bf16[64,64,896]{2,1,0:T(8,128)(2,1)} %param.13, s32[1024]{0:T(1024)S(1)} %pad_clamp_fusion.1), kind=kCustom, calls=%fused_computation | custom fusion | bytes 7340160 | tf_op jit(solution)/shard_map/jit(_take)/gather | solution.py:484
  27.6 0.0 copy-start
  27.6 6.7 %all-to-all-start = ((bf16[16,128,896]{2,1,0:T(8,128)(2,1)}), bf16[16,128,896]{2,1,0:T(8,128)(2,1)}, u32[]{:S(2)}, u32[]{:S(2)}) async-start(bf16[16,128,896]{2,1,0:T(8,128)(2,1)} %bitcast.23), calls=%async_computation | async-start | bytes 7340032 | tf_op jit(solution)/shard_map/all_to_all | solution.py:486
  34.3 0.0 all-gather.2.cloned.1.call-start
  34.3 0.0 copy-done
  34.4 0.1 reshape.46
  34.4 42.3 %shard_map.129 = (bf16[128,4096]{1,0:T(8,128)(2,1)}, bf16[512,1024]{1,0:T(8,128)(2,1)}) custom-call(bf16[128,2048]{1,0:T(8,128)(2,1)} %grad_ref), custom_call_target="tpu_custom_call" | custom-call | bytes 40000000 | tf_op jit(solution)/shard_map/pallas_call | solution.py:411
  76.8 12.6 %convolution_convert_fusion.5.dm_ref = bf16[128,2048]{1,0:T(8,128)(2,1)} fusion(bf16[128,4096]{1,0:T(8,128)(2,1)} %get-tuple-element.20, bf16[2048,4096]{1,0:T(8,128)(2,1)} %param.12), kind=kOutput, calls=%fused_computation.12 | convolution fusion | flops 2147745792 | bytes 18350080 | tf_op jit(solution)/shard_map/dot_general | solution.py:488
  89.3 15.0 %all-to-all-done = bf16[16,128,896]{2,1,0:T(8,128)(2,1)} async-done(((bf16[16,128,896]{2,1,0:T(8,128)(2,1)}), bf16[16,128,896]{2,1,0:T(8,128)(2,1)}, u32[]{:S(2)}, u32[]{:S(2)}) %all-to-all-start) | async-done | bytes 3670048 | tf_op jit(solution)/shard_map/all_to_all | solution.py:486
  104.4 4.0 %gather_fusion.1 = bf16[16,64,896]{2,1,0:T(8,128)(2,1)} fusion(bf16[32,64,896]{2,1,0:T(8,128)(2,1)} %bitcast.2, s32[1024]{0:T(1024)S(1)} %pad_clamp_fusion), kind=kCustom, calls=%fused_computation.1 | custom fusion | bytes 3670080 | tf_op jit(solution)/shard_map/jit(_take)/gather | solution.py:494
  108.4 7.2 %shard_map.130 = bf16[16,128,896]{2,1,0:T(8,128)(2,1)} custom-call(bf16[16,64,896]{2,1,0:T(8,128)(2,1)} %gather_fusion.1), custom_call_target="tpu_custom_call" | custom-call | tf_op jit(solution)/shard_map/pallas_call | solution.py:452
  115.6 19.7 %shard_map.131 = (bf16[128,2048]{1,0:T(8,128)(2,1)}, bf16[4,2,256,1024]{3,2,1,0:T(8,128)(2,1)}, bf16[16,128,896]{2,1,0:T(8,128)(2,1)}) custom-call(s32[2]{0:T(128)} %count_ref.1, bf16[2,1024,896]{2,1,0:T(8,128)(2,1)} %bitcast.25, bf16[128,2048]{1,0:T(8,128)(2,1)} %q_ref.3, bf16[896,2048]{1,0:T(8,128)(2,1)} %wk_ref.3, bf16[896,2048]{1,0:T(8,128)(2,1)} %wv_ref.3), custom_call_target="tpu_custom_call" | custom-call | flops 9019430912 | bytes 20000000 | tf_op jit(solution)/shard_map/pallas_call | solution.py:129
  135.3 0.0 all-gather.2.cloned.1.call-update
  135.3 0.0 reduce-scatter.2.cloned.1.call-start
  135.4 9.3 %convolution_convert_fusion = bf16[128,4096]{1,0:T(8,128)(2,1)} fusion(bf16[128,2048]{1,0:T(8,128)(2,1)} %get-tuple-element.23, bf16[2048,4096]{1,0:T(8,128)(2,1)} %param.12), kind=kOutput, calls=%fused_computation.2 | convolution fusion | flops 2148007936 | bytes 18350080 | tf_op jit(solution)/shard_map/dot_general | solution.py:498
  144.7 0.0 reduce-scatter.2.cloned.1.call-update
  144.7 0.0 copy-start.2
  144.7 23.1 %shard_map.132 = (bf16[128,2048]{1,0:T(8,128)(2,1)}, bf16[16,112,2048]{2,1,0:T(8,128)(2,1)}) custom-call(bf16[2,1024,896]{2,1,0:T(8,128)(2,1)} %bitcast.26, bf16[128,2048]{1,0:T(8,128)(2,1)} %q_ref.3, bf16[128,2048]{1,0:T(8,128)(2,1)} %convolution_convert_fusion.5.dm_ref, bf16[896,2048]{1,0:T(8,128)(2,1)} %wk_ref.3, bf16[896,2048]{1,0:T(8,128)(2,1)} %wv_ref.3, ...), custom_call_target="tpu_custom_call" | custom-call | flops 9019430912 | bytes 20000000 | tf_op jit(solution)/shard_map/pallas_call | solution.py:144
  167.8 13.1 %all-gather.2.cloned.1.call-done = bf16[512,2048]{1,0:T(8,128)(2,1)} async-done(((bf16[128,2048]{1,0:T(8,128)(2,1)}), bf16[512,2048]{1,0:T(8,128)(2,1)}) %all-gather.2.cloned.1.call-update) | async-done | bytes 2097168 | tf_op jit(solution)/shard_map/all_gather | solution.py:497
  180.9 0.0 copy-done.2
  180.9 0.0 copy-start.1
  180.9 2.5 fusion.3
  183.4 0.0 copy-done.1
  183.4 0.8 fusion.2
  184.2 0.8 fusion.1
  185.0 0.8 fusion
  185.7 2.3 pad_maximum_fusion
  188.1 124.4 %shard_map.133 = (f32[56,2048]{1,0:T(8,128)}, f32[56,2048]{1,0:T(8,128)}, f32[2048,256]{1,0:T(8,128)}) custom-call(bf16[2,2,2,2,112,2048]{5,4,3,2,1,0:T(8,128)(2,1)} %bitcast.24, bf16[2,2,2048,256]{3,2,1,0:T(8,128)(2,1)} %bitcast.22), custom_call_target="tpu_custom_call" | custom-call | flops 3670016 | bytes 300000000 | tf_op jit(solution)/shard_map/pallas_call | solution.py:299
  312.5 0.0 reduce-scatter.2.cloned.1.call-done
  312.5 1.8 copy.19
  314.4 1.8 copy.20
  316.2 3.0 copy.21
  (4 shorter events, 0.0 us)
Async XLA Ops:
  27.6 6.8 %copy-start = (s32[2,8]{1,0:T(2,128)S(1)}, s32[2,8]{1,0:T(2,128)}, u32[]{:S(2)}) copy-start(s32[2,8]{1,0:T(2,128)} %param.15) | copy-start | bytes 196
  27.6 76.8 %all-to-all-start = ((bf16[16,128,896]{2,1,0:T(8,128)(2,1)}), bf16[16,128,896]{2,1,0:T(8,128)(2,1)}, u32[]{:S(2)}, u32[]{:S(2)}) async-start(bf16[16,128,896]{2,1,0:T(8,128)(2,1)} %bitcast.23), calls=%async_computation | async-start | bytes 7340032 | tf_op jit(solution)/shard_map/all_to_all | solution.py:486
  34.3 146.6 %all-gather.2.cloned.1.call-start = ((), (), s32[]{:S(2)}) async-start(), calls=%async_computation.3 | async-start | bytes 2621440 | tf_op jit(solution)/shard_map/all_gather | solution.py:497
  135.3 177.2 %reduce-scatter.2.cloned.1.call-start = ((), (), s32[]{:S(2)}) async-start(), calls=%async_computation.2 | async-start | bytes 1572864 | tf_op jit(solution)/shard_map/reduce_scatter | solution.py:499
  144.7 36.2 %copy-start.2 = (bf16[512,1024]{1,0:T(8,128)(2,1)S(1)}, bf16[512,1024]{1,0:T(8,128)(2,1)}, u32[]{:S(2)}) copy-start(bf16[512,1024]{1,0:T(8,128)(2,1)} %get-tuple-element.29) | copy-start | bytes 3145732
  180.9 2.5 copy-start.1
Sparse Core Ops, SparseCore 0:
  135.4 45.4 all-gather.1
Sparse Core Ops, SparseCore 1:
  144.8 18.6 reduce-scatter.1

commit v5 on v4

--- a/solution.py
+++ b/solution.py
@@ -263,14 +263,13 @@
         k = len(copies)
         copies.append(track.start(send_sem.at[k], recv_sem.at[k]))
 
-    for pair in rounds[0:2] + rounds[3::2] + rounds[2:3]:
-        for track in pair:
-            start(track)
+    for track in rounds[0]:
+        start(track)
     active = []
     for t in range(len(rounds) + all_bits):
         active += rounds[t:t + 1]
-        if t % 2 == 0 and t + 4 < len(rounds):
-            for track in rounds[t + 4]:
+        for pair in rounds[t + 1:t + 2]:
+            for track in pair:
                 start(track)
         for pair in list(active):
             for track in pair:

time: 329 us -> 319 us (0.970)
  Pallas kernels: 228 us -> 220 us
    pallas_call x1, Pallas kernels: 124 us -> 117 us  [reduce_scatter(): pl.pallas_call(functools.partial(reduce_kernel, all_bits, wo_bits), in_sp...]
  transfers between devices with their start and end apart: 3 -> 3, of which waited for: 2 -> 2; matrix products, arithmetic and copies ran while one was open for 9% -> 9% of each run, Pallas kernels for 58% -> 57%
where the time goes in v5:
time: 319 us
  Pallas kernels  220 us (69%)
  waiting for transfers between devices  28.2 us (9%)
  matrix products  26.6 us (8%)
  local copies, waits for them, and re-layouts  18.3 us (6%)
  between operations  15.6 us (5%)
  starting transfers between devices  6.8 us (2%)
    pallas_call x1, Pallas kernels, reduce_scatter(): pl.pallas_call(functools.partial(reduce_kernel, all_bits, wo_bits), in_sp...  117 us
    pallas_call x1, Pallas kernels, exchange(): pl.pallas_call(functools.partial(exchange_kernel, low), in_specs=[in_vmem...  42.3 us
    pallas_call x1, Pallas kernels, attend_back(): pl.pallas_call(functools.partial(backward_kernel, groups, heads, shares),...  23.1 us
    pallas_call x1, Pallas kernels, attend(): pl.pallas_call(functools.partial(forward_kernel, groups, heads), in_specs...  19.7 us
    all_to_all x1, waiting for transfers between devices, shards(): lax.all_to_all(table, 'db', split_axis=0, concat_axis=0, tiled=True)  15 us
    all_gather x1, waiting for transfers between devices, shards(): lax.all_gather(mixed, 'db', axis=0, axis_index_groups=planes, tiled=True)  13.1 us
    dot_general x1, matrix products, shards(): lax.dot_general(piece, w_out, (((1,), (1,)), ((), ())), preferred_element...  12.6 us
    pallas_call x1, Pallas kernels, request(): pl.pallas_call(request_kernel, in_specs=[in_vmem], out_specs=in_vmem, out...  11.2 us
  transfers between devices with their start and end apart: 3, of which 2 were waited for; matrix products, arithmetic and copies ran while one was open for 9% of the time, Pallas kernels for 57%

profile of v5, /device:TPU:0, one launch (start us, length us, event | category | flops | bytes accessed | tf_op | source)
XLA Modules:
  0.0 318.7 jit_solution(5189508578409536085)
XLA Ops:
  8.0 0.8 select_reduce_fusion
  8.8 0.1 copy.15
  8.9 0.6 broadcast_in_dim.30.wanted_ref
  9.5 11.2 %shard_map.128 = s32[16,8,128]{2,1,0:T(8,128)} custom-call(s32[16,8,128]{2,1,0:T(8,128)} %broadcast_in_dim.30.wanted_ref), custom_call_target="tpu_custom_call" | custom-call | tf_op jit(solution)/shard_map/pallas_call | solution.py:394
  20.7 0.9 slice_reduce_fusion
  21.6 0.1 reshape.38
  21.7 5.9 %gather_fusion = bf16[32,64,896]{2,1,0:T(8,128)(2,1)} fusion(bf16[64,64,896]{2,1,0:T(8,128)(2,1)} %param.13, s32[1024]{0:T(1024)S(1)} %pad_clamp_fusion.1), kind=kCustom, calls=%fused_computation | custom fusion | bytes 7340160 | tf_op jit(solution)/shard_map/jit(_take)/gather | solution.py:483
  27.6 0.0 copy-start
  27.6 6.7 %all-to-all-start = ((bf16[16,128,896]{2,1,0:T(8,128)(2,1)}), bf16[16,128,896]{2,1,0:T(8,128)(2,1)}, u32[]{:S(2)}, u32[]{:S(2)}) async-start(bf16[16,128,896]{2,1,0:T(8,128)(2,1)} %bitcast.23), calls=%async_computation | async-start | bytes 7340032 | tf_op jit(solution)/shard_map/all_to_all | solution.py:485
  34.3 0.0 all-gather.2.cloned.1.call-start
  34.3 0.0 copy-done
  34.4 0.1 reshape.46
  34.4 42.3 %shard_map.129 = (bf16[128,4096]{1,0:T(8,128)(2,1)}, bf16[512,1024]{1,0:T(8,128)(2,1)}) custom-call(bf16[128,2048]{1,0:T(8,128)(2,1)} %grad_ref), custom_call_target="tpu_custom_call" | custom-call | bytes 40000000 | tf_op jit(solution)/shard_map/pallas_call | solution.py:410
  76.8 12.6 %convolution_convert_fusion.5.dm_ref = bf16[128,2048]{1,0:T(8,128)(2,1)} fusion(bf16[128,4096]{1,0:T(8,128)(2,1)} %get-tuple-element.20, bf16[2048,4096]{1,0:T(8,128)(2,1)} %param.12), kind=kOutput, calls=%fused_computation.12 | convolution fusion | flops 2147745792 | bytes 18350080 | tf_op jit(solution)/shard_map/dot_general | solution.py:487
  89.3 15.0 %all-to-all-done = bf16[16,128,896]{2,1,0:T(8,128)(2,1)} async-done(((bf16[16,128,896]{2,1,0:T(8,128)(2,1)}), bf16[16,128,896]{2,1,0:T(8,128)(2,1)}, u32[]{:S(2)}, u32[]{:S(2)}) %all-to-all-start) | async-done | bytes 3670048 | tf_op jit(solution)/shard_map/all_to_all | solution.py:485
  104.4 4.0 %gather_fusion.1 = bf16[16,64,896]{2,1,0:T(8,128)(2,1)} fusion(bf16[32,64,896]{2,1,0:T(8,128)(2,1)} %bitcast.2, s32[1024]{0:T(1024)S(1)} %pad_clamp_fusion), kind=kCustom, calls=%fused_computation.1 | custom fusion | bytes 3670080 | tf_op jit(solution)/shard_map/jit(_take)/gather | solution.py:493
  108.4 7.2 %shard_map.130 = bf16[16,128,896]{2,1,0:T(8,128)(2,1)} custom-call(bf16[16,64,896]{2,1,0:T(8,128)(2,1)} %gather_fusion.1), custom_call_target="tpu_custom_call" | custom-call | tf_op jit(solution)/shard_map/pallas_call | solution.py:451
  115.6 19.7 %shard_map.131 = (bf16[128,2048]{1,0:T(8,128)(2,1)}, bf16[4,2,256,1024]{3,2,1,0:T(8,128)(2,1)}, bf16[16,128,896]{2,1,0:T(8,128)(2,1)}) custom-call(s32[2]{0:T(128)} %count_ref.1, bf16[2,1024,896]{2,1,0:T(8,128)(2,1)} %bitcast.25, bf16[128,2048]{1,0:T(8,128)(2,1)} %q_ref.3, bf16[896,2048]{1,0:T(8,128)(2,1)} %wk_ref.3, bf16[896,2048]{1,0:T(8,128)(2,1)} %wv_ref.3), custom_call_target="tpu_custom_call" | custom-call | flops 9019430912 | bytes 20000000 | tf_op jit(solution)/shard_map/pallas_call | solution.py:129
  135.3 0.0 all-gather.2.cloned.1.call-update
  135.3 0.0 reduce-scatter.2.cloned.1.call-start
  135.4 9.3 %convolution_convert_fusion = bf16[128,4096]{1,0:T(8,128)(2,1)} fusion(bf16[128,2048]{1,0:T(8,128)(2,1)} %get-tuple-element.23, bf16[2048,4096]{1,0:T(8,128)(2,1)} %param.12), kind=kOutput, calls=%fused_computation.2 | convolution fusion | flops 2148007936 | bytes 18350080 | tf_op jit(solution)/shard_map/dot_general | solution.py:497
  144.7 0.0 reduce-scatter.2.cloned.1.call-update
  144.7 0.0 copy-start.2
  144.7 23.1 %shard_map.132 = (bf16[128,2048]{1,0:T(8,128)(2,1)}, bf16[16,112,2048]{2,1,0:T(8,128)(2,1)}) custom-call(bf16[2,1024,896]{2,1,0:T(8,128)(2,1)} %bitcast.26, bf16[128,2048]{1,0:T(8,128)(2,1)} %q_ref.3, bf16[128,2048]{1,0:T(8,128)(2,1)} %convolution_convert_fusion.5.dm_ref, bf16[896,2048]{1,0:T(8,128)(2,1)} %wk_ref.3, bf16[896,2048]{1,0:T(8,128)(2,1)} %wv_ref.3, ...), custom_call_target="tpu_custom_call" | custom-call | flops 9019430912 | bytes 20000000 | tf_op jit(solution)/shard_map/pallas_call | solution.py:144
  167.8 13.1 %all-gather.2.cloned.1.call-done = bf16[512,2048]{1,0:T(8,128)(2,1)} async-done(((bf16[128,2048]{1,0:T(8,128)(2,1)}), bf16[512,2048]{1,0:T(8,128)(2,1)}) %all-gather.2.cloned.1.call-update) | async-done | bytes 2097168 | tf_op jit(solution)/shard_map/all_gather | solution.py:496
  180.9 0.0 copy-done.2
  180.9 0.0 copy-start.1
  180.9 2.5 fusion.3
  183.4 0.0 copy-done.1
  183.4 0.8 fusion.2
  184.2 0.8 fusion.1
  185.0 0.8 fusion
  185.7 2.3 pad_maximum_fusion
  188.1 116.5 %shard_map.133 = (f32[56,2048]{1,0:T(8,128)}, f32[56,2048]{1,0:T(8,128)}, f32[2048,256]{1,0:T(8,128)}) custom-call(bf16[2,2,2,2,112,2048]{5,4,3,2,1,0:T(8,128)(2,1)} %bitcast.24, bf16[2,2,2048,256]{3,2,1,0:T(8,128)(2,1)} %bitcast.22), custom_call_target="tpu_custom_call" | custom-call | flops 3670016 | bytes 300000000 | tf_op jit(solution)/shard_map/pallas_call | solution.py:298
  304.6 0.0 reduce-scatter.2.cloned.1.call-done
  304.6 1.8 copy.19
  306.4 1.8 copy.20
  308.3 3.0 copy.21
  (4 shorter events, 0.0 us)
Async XLA Ops:
  27.6 6.8 %copy-start = (s32[2,8]{1,0:T(2,128)S(1)}, s32[2,8]{1,0:T(2,128)}, u32[]{:S(2)}) copy-start(s32[2,8]{1,0:T(2,128)} %param.15) | copy-start | bytes 196
  27.6 76.8 %all-to-all-start = ((bf16[16,128,896]{2,1,0:T(8,128)(2,1)}), bf16[16,128,896]{2,1,0:T(8,128)(2,1)}, u32[]{:S(2)}, u32[]{:S(2)}) async-start(bf16[16,128,896]{2,1,0:T(8,128)(2,1)} %bitcast.23), calls=%async_computation | async-start | bytes 7340032 | tf_op jit(solution)/shard_map/all_to_all | solution.py:485
  34.3 146.6 %all-gather.2.cloned.1.call-start = ((), (), s32[]{:S(2)}) async-start(), calls=%async_computation.3 | async-start | bytes 2621440 | tf_op jit(solution)/shard_map/all_gather | solution.py:496
  135.3 169.3 %reduce-scatter.2.cloned.1.call-start = ((), (), s32[]{:S(2)}) async-start(), calls=%async_computation.2 | async-start | bytes 1572864 | tf_op jit(solution)/shard_map/reduce_scatter | solution.py:498
  144.7 36.2 %copy-start.2 = (bf16[512,1024]{1,0:T(8,128)(2,1)S(1)}, bf16[512,1024]{1,0:T(8,128)(2,1)}, u32[]{:S(2)}) copy-start(bf16[512,1024]{1,0:T(8,128)(2,1)} %get-tuple-element.29) | copy-start | bytes 3145732
  180.9 2.5 copy-start.1
Sparse Core Ops, SparseCore 0:
  135.4 45.4 all-gather.1
Sparse Core Ops, SparseCore 1:
  144.8 18.6 reduce-scatter.1
